TPU v7x, 128 devices: a whole 4x4x4 slice. The times are simulated.
128 devices in a mesh: gx: 8 (over z, core), yz: 16 (over y, x).
Axes of the slice: x: 4, y: 4, z: 4, core: 2. Of those that a mesh axis runs over, the one named last changes fastest.
Arguments:
- mixture_fractions: float32 [53, 64, 128, 256], P(None, 'gx', 'yz'), may hold values from 0 to 0.2
- thermal_kelvins: float32 [64, 128, 256], P('gx', 'yz'), may hold values from 300 to 2400
- normalized_thrust_load: float32 [64, 128, 256], P('gx', 'yz'), may hold values from 0.85 to 1.15
- fluid_motion_vector: float32 [3, 64, 128, 256], P(None, 'gx', 'yz'), as said below
- diffusion_coefficient: float32 [54], replicated, may hold values from 0.01 to 0.1
- burning_tally: int32 [8, 16], P('gx', 'yz'), may hold values from 1 to 4096, 32768 in all within a row
- burning_location_list: int32 [8, 16, 4096], P('gx', 'yz'), may hold values from 0 to 16383, as said below
- opening_matrix: bfloat16 [55, 1600], replicated, may hold values from -0.875 to 0.875
- opening_offset: float32 [1600], replicated, may hold values from -3 to 3
- secondary_matrix: bfloat16 [1600, 800], replicated, may hold values from -0.15625 to 0.15625
- secondary_offset: float32 [800], replicated, may hold values from -3 to 3
- tertiary_matrix: bfloat16 [800, 400], replicated, may hold values from -0.21875 to 0.21875
- tertiary_offset: float32 [400], replicated, may hold values from -3 to 3
- closing_matrix: bfloat16 [400, 53], replicated, may hold values from -0.3125 to 0.3125
- closing_offset: float32 [53], replicated, may hold values from -3 to 3
- increment_magnitude: float32 [53], replicated, may hold values from 0.002 to 0.02
- formation_heat_ratio: float32 [53], replicated, may hold values from -12288 to 12288
Outputs:
- species_next: float32 [53, 64, 128, 256], P(None, 'gx', 'yz')
- temperature_next: float32 [64, 128, 256], P('gx', 'yz')
Inputs may be any that keep to these rules, and one draw needn't show every extreme that they name: In each mesh block the 4096 entries of burning_location_list are distinct cell numbers of that block. `burning_tally`: the counts of each row of mesh blocks along yz sum to exactly 2048 times the number of blocks along yz; some block in each such row holds exactly 4096. `fluid_motion_vector`: the velocities' typical magnitude grows toward the upstream end of the jet (gx index 0); single values are random.
All inputs are finite; a program needn't handle non-finite values. Where the computation divides by a largest or mean magnitude, that divisor is 1e-20 or more.
Results may differ from a plain program's by a relative error of at most 0.0004.
Values may be sent and summed in bfloat16 or wider, within the bound.
A program may use at most 128 MiB of HBM per device.

v0:
```python
import jax
import jax.numpy as jnp
from jax import lax
from jax.sharding import PartitionSpec as P


def with_halo(block, sides, width):
    for axis, dim in sides:
        count = lax.axis_size(axis)
        forward = [(i, i + 1) for i in range(count - 1)]
        backward = [(target, source) for source, target in forward]
        low = lax.ppermute(
            lax.slice_in_dim(block, block.shape[dim] - width, None, axis=dim), axis, forward
        )
        high = lax.ppermute(lax.slice_in_dim(block, 0, width, axis=dim), axis, backward)
        block = jnp.concatenate([low, block, high], axis=dim)
    return block


def upwind(speed, left, right):
    return jnp.where(speed > 0, speed * left, speed * right)


def advance(padded, vel, diffusion_coefficient, step):
    centre = padded[:, 1:-1, 1:-1]
    uc = vel[:, 1:-1, 1:-1]
    xplus = padded[:, 2:, 1:-1]
    xminus = padded[:, :-2, 1:-1]
    yplus = padded[:, 1:-1, 2:]
    yminus = padded[:, 1:-1, :-2]
    zplus = jnp.roll(centre, -1, 3)
    zminus = jnp.roll(centre, 1, 3)
    flux_x = upwind(0.5 * (uc[0] + vel[0, 2:, 1:-1]), centre, xplus) - upwind(
        0.5 * (vel[0, :-2, 1:-1] + uc[0]), xminus, centre
    )
    flux_y = upwind(0.5 * (uc[1] + vel[1, 1:-1, 2:]), centre, yplus) - upwind(
        0.5 * (vel[1, 1:-1, :-2] + uc[1]), yminus, centre
    )
    flux_z = upwind(0.5 * (uc[2] + jnp.roll(uc[2], -1, 2)), centre, zplus) - upwind(
        0.5 * (jnp.roll(uc[2], 1, 2) + uc[2]), zminus, centre
    )
    laplace = xplus + xminus + yplus + yminus + zplus + zminus - 6.0 * centre
    return centre + step * (
        diffusion_coefficient[:, None, None, None] * laplace - (flux_x + flux_y + flux_z)
    )


def normalize(rows):
    nspec = rows.shape[-1] - 2
    centre = jnp.concatenate(
        [jnp.full((nspec,), 0.1, jnp.float32), jnp.array([1350.0, 1.0], jnp.float32)]
    )
    spread = jnp.concatenate(
        [jnp.full((nspec,), 0.06, jnp.float32), jnp.array([600.0, 0.1], jnp.float32)]
    )
    return ((rows - centre) / spread).astype(jnp.bfloat16)


def chemistry(
    inputs,
    opening_matrix,
    opening_offset,
    secondary_matrix,
    secondary_offset,
    tertiary_matrix,
    tertiary_offset,
    closing_matrix,
    closing_offset,
    increment_magnitude,
    formation_heat_ratio,
):
    hidden = jax.nn.gelu(
        jnp.dot(inputs, opening_matrix, preferred_element_type=jnp.float32) + opening_offset
    ).astype(jnp.bfloat16)
    hidden = jax.nn.gelu(
        jnp.dot(hidden, secondary_matrix, preferred_element_type=jnp.float32) + secondary_offset
    ).astype(jnp.bfloat16)
    hidden = jax.nn.gelu(
        jnp.dot(hidden, tertiary_matrix, preferred_element_type=jnp.float32) + tertiary_offset
    ).astype(jnp.bfloat16)
    delta = (
        jnp.dot(hidden, closing_matrix, preferred_element_type=jnp.float32) + closing_offset
    ) * increment_magnitude
    heat = -jnp.dot(delta, formation_heat_ratio, precision=lax.Precision.HIGHEST)
    return jnp.concatenate([delta, heat[:, None]], axis=1)


def shards(
    mixture_fractions,
    thermal_kelvins,
    normalized_thrust_load,
    fluid_motion_vector,
    diffusion_coefficient,
    burning_tally,
    burning_location_list,
    opening_matrix,
    opening_offset,
    secondary_matrix,
    secondary_offset,
    tertiary_matrix,
    tertiary_offset,
    closing_matrix,
    closing_offset,
    increment_magnitude,
    formation_heat_ratio,
):
    nspec, depth_x, depth_y, depth_z = mixture_fractions.shape
    ncells = depth_x * depth_y * depth_z
    weights = (
        opening_matrix,
        opening_offset,
        secondary_matrix,
        secondary_offset,
        tertiary_matrix,
        tertiary_offset,
        closing_matrix,
        closing_offset,
        increment_magnitude,
        formation_heat_ratio,
    )
    network_features = jnp.concatenate(
        [mixture_fractions, thermal_kelvins[None], fluid_motion_vector], 0
    )
    padded = with_halo(network_features, (("gx", 1), ("yz", 2)), 1)
    fastest = lax.pmax(jnp.max(jnp.sum(jnp.abs(fluid_motion_vector), axis=0)), ("gx", "yz"))
    step = 0.9 / (fastest + 6.0 * jnp.max(diffusion_coefficient))
    fluid_snapshot = jnp.concatenate(
        [mixture_fractions, thermal_kelvins[None], normalized_thrust_load[None]], 0
    ).reshape(nspec + 2, ncells)
    index = burning_location_list[0, 0]
    count = burning_tally[0, 0]
    capacity = index.shape[0]
    inputs = normalize(jnp.take(fluid_snapshot, index, axis=1).T)
    slots = jnp.arange(capacity, dtype=jnp.int32)
    valid = slots < count
    result = chemistry(inputs, *weights)
    result = result * valid[:, None].astype(jnp.float32)
    change = jnp.zeros((nspec + 1, ncells), jnp.float32).at[:, index].add(result.T)
    moved = advance(padded[: nspec + 1], padded[nspec + 1 :], diffusion_coefficient, step)
    final = moved + change.reshape(nspec + 1, depth_x, depth_y, depth_z)
    return (final[:nspec], final[nspec])


def solution(mesh):
    in_specs = (
        P(None, "gx", "yz", None),
        P("gx", "yz", None),
        P("gx", "yz", None),
        P(None, "gx", "yz", None),
        P(),
        P("gx", "yz"),
        P("gx", "yz", None),
        P(),
        P(),
        P(),
        P(),
        P(),
        P(),
        P(),
        P(),
        P(),
        P(),
    )
    out_specs = (P(None, "gx", "yz", None), P("gx", "yz", None))
    return jax.shard_map(shards, mesh=mesh, in_specs=in_specs, out_specs=out_specs, check_vma=False)
```

profile of v0, /device:TPU:1, one launch (start us, length us, event | category | flops | bytes accessed | tf_op | source)
XLA Modules:
  0.0 234.3 jit_solution(17237610817598244678)
XLA Ops:
  0.7 2.4 %pad_maximum_fusion.12 = (f32[57,1,8,256]{3,2,1,0:T(8,128)}, f32[57,1,8,256]{3,2,1,0:T(8,128)}) fusion(f32[3,8,8,256]{3,2,1,0:T(8,128)} %param.22, f32[1,8,8,256]{3,2,1,0:T(8,128)} %bitcast.63, f32[53,8,8,256]{3,2,1,0:T(8,128)} %param.19), kind=kLoop, calls=%fused_computation.70 | loop fusion | flops 466944 | bytes 4669440 | tf_op jit(solution)/shard_map/concatenate | solution.py:121
  3.0 3.3 %collective-permute-start = (f32[57,1,8,256]{3,2,1,0:T(8,128)}, f32[57,1,8,256]{3,2,1,0:T(8,128)}, u32[]{:S(2)}, u32[]{:S(2)}) collective-permute-start(f32[57,1,8,256]{3,2,1,0:T(8,128)} %get-tuple-element.27), channel_id=1, source_target_pairs={{16,0},{32,16},{48,32},{64,48},{80,64},{96,80},{112,96},{17,1},{33... | collective-permute-start | bytes 1400840 | tf_op jit(solution)/shard_map/ppermute | solution.py:15
  6.4 3.5 %collective-permute-start.1 = (f32[57,1,8,256]{3,2,1,0:T(8,128)}, f32[57,1,8,256]{3,2,1,0:T(8,128)S(1)}, u32[]{:S(2)}, u32[]{:S(2)}) collective-permute-start(f32[57,1,8,256]{3,2,1,0:T(8,128)} %get-tuple-element.26), channel_id=1, source_target_pairs={{0,16},{16,32},{32,48},{48,64},{64,80},{80,96},{96,112},{1,17},{17... | collective-permute-start | bytes 1400840 | tf_op jit(solution)/shard_map/ppermute | solution.py:12
  13.6 2.4 %pad.98 = f32[56,64,256]{2,1,0:T(8,128)S(1)} pad(f32[53,64,256]{2,1,0:T(8,128)} %bitcast.59, f32[]{:T(128)} %constant.17.clone.1), padding=0_3x0_0x0_0 | pad | bytes 7143428
  16.0 2.1 copy.152
  18.1 2.1 pad_maximum_fusion.2
  20.3 6.9 %copy.148 = f32[55,16384]{0,1:T(8,128)} copy(f32[55,16384]{1,0:T(8,128)} %pad_maximum_fusion.2) | data formatting | bytes 7208960 | tf_op jit(solution)/shard_map/concatenate | solution.py:127
  27.2 17.6 %gather_fusion = f32[4096,55]{1,0:T(8,128)} fusion(f32[55,16384]{0,1:T(8,128)} %copy.148, s32[4096]{0:T(1024)S(1)} %broadcast_clamp_fusion), kind=kCustom, calls=%fused_computation | custom fusion | bytes 1818624 | tf_op jit(solution)/shard_map/jit(_take)/gather | solution.py:133
  44.8 12.0 %fusion.7.clone.4 = bf16[4096,1600]{0,1:T(8,128)(2,1)S(1)} fusion(bf16[55,1600]{1,0:T(8,128)(2,1)} %param.26, f32[1600]{0:T(1024)S(1)} %copy-done.26, f32[4096,55]{1,0:T(8,128)} %gather_fusion, f32[55]{0:T(128)S(1)} %copy-done.31, f32[55]{0:T(128)S(1)} %copy-done.32, pred[4096]{0:T(1024)(128)(4,1)S(1)} %compare_and_fusion), kind=kOutput, calls=%fused_computation.10.clone.clone.clone.1 | convolution fusion | flops 787333120 | bytes 14195256 | tf_op jit(solution)/shard_map/dot_general | solution.py:73
  56.9 15.0 %fusion.8 = f32[4096,800]{0,1:T(8,128)} fusion(bf16[1600,800]{0,1:T(8,128)(2,1)S(1)} %copy-done, bf16[4096,1600]{0,1:T(8,128)(2,1)S(1)} %fusion.7.clone.4), kind=kOutput, calls=%fused_computation.12 | convolution fusion | flops 10485760000 | bytes 28774400 | tf_op jit(solution)/shard_map/dot_general | solution.py:76
  72.0 11.1 %fusion.32 = f32[4096,53]{0,1:T(8,128)S(1)} fusion(bf16[400,53]{0,1:T(8,128)(2,1)S(1)} %copy-done.25, bf16[800,400]{0,1:T(8,128)(2,1)} %param.30, f32[4096,800]{0,1:T(8,128)} %fusion.8, f32[800]{0:T(1024)S(1)} %copy-done.27, f32[400]{0:T(512)S(1)} %copy-done.28, f32[53]{0:T(128)S(1)} %copy-done.29, f32[53]{0:T(128)S(1)} %copy-done.30), kind=kOutput, calls=%fused_computation.42 | convolution fusion | flops 2844696576 | bytes 14663176 | tf_op jit(solution)/shard_map/dot_general | solution.py:82
  86.0 6.1 %fusion.37 = (f32[54,8,8,255]{3,2,1,0:T(8,128)}, f32[54,8,8,255]{3,2,1,0:T(8,128)}) fusion(f32[1,8,8,256]{3,2,1,0:T(8,128)S(1)} %bitcast.64, f32[53,8,8,256]{3,2,1,0:T(8,128)} %param.19), kind=kLoop, calls=%fused_computation.48 | loop fusion | flops 1762560 | bytes 10589184 | tf_op jit(solution)/shard_map/concatenate | solution.py:121
  92.1 2.8 %pad_maximum_fusion.11 = (f32[57,10,1,256]{3,2,1,0:T(1,128)}, f32[57,10,1,256]{3,2,1,0:T(1,128)}) fusion(f32[57,1,8,256]{3,2,1,0:T(8,128)} %collective-permute-done, f32[57,1,8,256]{3,2,1,0:T(8,128)S(1)} %collective-permute-done.1, f32[3,8,8,256]{3,2,1,0:T(8,128)S(1)} %copy-done.4, f32[1,8,8,256]{3,2,1,0:T(8,128)S(1)} %bitcast.65, ...), kind=kLoop, calls=%fused_computation.69 | loop fusion | flops 1167360 | bytes 5836800 | tf_op jit(solution)/shard_map/slice | solution.py:15
  94.9 3.1 %collective-permute-start.3 = (f32[57,10,1,256]{3,2,1,0:T(1,128)}, f32[57,10,1,256]{3,2,1,0:T(1,128)S(1)}, u32[]{:S(2)}, u32[]{:S(2)}) collective-permute-start(f32[57,10,1,256]{3,2,1,0:T(1,128)} %get-tuple-element.19), channel_id=1, source_target_pairs={{0,1},{1,2},{2,3},{3,4},{4,5},{5,6},{6,7},{7,8},{8,9},{9,10},{10,1... | collective-permute-start | bytes 1751048 | tf_op jit(solution)/shard_map/ppermute | solution.py:12
  98.0 1.3 collective-permute-start.2
  99.3 2.4 %fusion.39 = (f32[54,8,8,1]{3,2,1,0:T(8,128)}, f32[54,8,8,1]{3,2,1,0:T(8,128)}) fusion(f32[53,8,8,256]{3,2,1,0:T(8,128)S(1)} %copy-done.2, f32[1,8,8,256]{3,2,1,0:T(8,128)S(1)} %bitcast.66), kind=kLoop, calls=%fused_computation.58 | loop fusion | flops 6912 | bytes 3566592 | tf_op jit(solution)/shard_map/concatenate | solution.py:121
  101.7 72.8 %pmax.7 = f32[]{:T(128)} all-reduce(f32[]{:T(128)} %reduce_max.18), channel_id=1, replica_groups=mesh['gx'=8,'yz'=16] {'gx','yz'}, use_global_device_ids=true, to_apply=%region_2.0 | all-reduce | flops 1 | bytes 8 | tf_op jit(solution)/shard_map/pmax | solution.py:125
  174.5 2.0 copy.149
  176.5 26.4 %scatter_custom_fusion = f32[54,16384]{0,1:T(8,128)} fusion(s32[4096]{0:T(1024)} %bitcast.78, f32[4096,54]{1,0:T(8,128)} %copy.149, f32[]{:T(128)} %constant.17.clone.1), kind=kCustom, calls=%fused_computation.45 | custom fusion | flops 221184 | bytes 3539456 | tf_op jit(solution)/shard_map/scatter-add | solution.py:138
  202.9 7.2 %copy.151 = f32[54,8,8,256]{3,2,1,0:T(8,128)} copy(f32[54,8,8,256]{0,3,2,1:T(8,128)} %bitcast.60) | data formatting | bytes 7077888 | tf_op jit(solution)/shard_map/reshape | solution.py:140
  212.1 3.8 %pad_maximum_fusion.1 = (f32[57,9,8,256]{3,2,1,0:T(8,128)S(1)}, f32[57,9,8,256]{3,2,1,0:T(8,128)S(1)}) fusion(f32[57,1,8,256]{3,2,1,0:T(8,128)} %collective-permute-done, f32[3,8,8,256]{3,2,1,0:T(8,128)S(1)} %copy-done.4, f32[1,8,8,256]{3,2,1,0:T(8,128)S(1)} %bitcast.68, f32[53,8,8,256]{3,2,1,0:T(8,128)} %param.19, ...), kind=kLoop, calls=%fused_computation.43 | loop fusion | flops 6303744 | bytes 13074432 | tf_op jit(solution)/shard_map/concatenate | solution.py:16
  216.3 1.7 compare_bitcast_fusion.3
  219.1 12.5 %add_add_fusion = f32[54,8,8,256]{3,2,1,0:T(8,128)S(1)} fusion(f32[54,8,8,256]{3,2,1,0:T(8,128)S(1)} %copy-done.5, f32[1,8,8,256]{3,2,1,0:T(8,128)S(1)} %bitcast.70, f32[54,8,8,255]{3,2,1,0:T(8,128)} %get-tuple-element.29, f32[54,8,8,1]{3,2,1,0:T(8,128)} %get-tuple-element.31, f32[54,8,8,1]{3,2,1,0:T(8,128)} %get-tuple-element.30, ...), kind=kLoop, calls=%fused_computation.54 | loop fusion | flops 42467328 | bytes 27562204 | tf_op jit(solution)/shard_map/add | solution.py:140
  231.6 2.0 slice.175
  (89 shorter events, 8.6 us)
Async XLA Ops:
  0.6 56.2 %copy-start = (bf16[1600,800]{0,1:T(8,128)(2,1)S(1)}, bf16[1600,800]{0,1:T(8,128)(2,1)}, u32[]{:S(2)}) copy-start(bf16[1600,800]{0,1:T(8,128)(2,1)} %param.28) | copy-start | bytes 7680004
  0.7 11.4 %copy-start.20 = (s32[1,1,4096]{2,1,0:T(1,128)S(1)}, s32[1,1,4096]{2,1,0:T(1,128)}, u32[]{:S(2)}) copy-start(s32[1,1,4096]{2,1,0:T(1,128)} %param.25) | copy-start | bytes 49156
  3.0 89.1 %collective-permute-start = (f32[57,1,8,256]{3,2,1,0:T(8,128)}, f32[57,1,8,256]{3,2,1,0:T(8,128)}, u32[]{:S(2)}, u32[]{:S(2)}) collective-permute-start(f32[57,1,8,256]{3,2,1,0:T(8,128)} %get-tuple-element.27), channel_id=1, source_target_pairs={{16,0},{32,16},{48,32},{64,48},{80,64},{96,80},{112,96},{17,1},{33... | collective-permute-start | bytes 1400840 | tf_op jit(solution)/shard_map/ppermute | solution.py:15
  6.4 85.7 %collective-permute-start.1 = (f32[57,1,8,256]{3,2,1,0:T(8,128)}, f32[57,1,8,256]{3,2,1,0:T(8,128)S(1)}, u32[]{:S(2)}, u32[]{:S(2)}) collective-permute-start(f32[57,1,8,256]{3,2,1,0:T(8,128)} %get-tuple-element.26), channel_id=1, source_target_pairs={{0,16},{16,32},{32,48},{48,64},{64,80},{80,96},{96,112},{1,17},{17... | collective-permute-start | bytes 1400840 | tf_op jit(solution)/shard_map/ppermute | solution.py:12
  27.2 17.6 %copy-start.26 = (f32[1600]{0:T(1024)S(1)}, f32[1600]{0:T(1024)}, u32[]{:S(2)}) copy-start(f32[1600]{0:T(1024)} %param.27) | copy-start | bytes 19204
  27.2 17.6 %copy-start.31 = (f32[55]{0:T(128)S(1)}, f32[55]{0:T(128)}, u32[]{:S(2)}) copy-start(f32[55]{0:T(128)} %constant.68) | copy-start | bytes 664
  27.2 17.6 %copy-start.32 = (f32[55]{0:T(128)S(1)}, f32[55]{0:T(128)}, u32[]{:S(2)}) copy-start(f32[55]{0:T(128)} %constant.69) | copy-start | bytes 664
  56.9 15.1 %copy-start.25 = (bf16[400,53]{0,1:T(8,128)(2,1)S(1)}, bf16[400,53]{0,1:T(8,128)(2,1)}, u32[]{:S(2)}) copy-start(bf16[400,53]{0,1:T(8,128)(2,1)} %param.32) | copy-start | bytes 127204
  56.9 15.0 %copy-start.27 = (f32[800]{0:T(1024)S(1)}, f32[800]{0:T(1024)}, u32[]{:S(2)}) copy-start(f32[800]{0:T(1024)} %param.29) | copy-start | bytes 9604
  56.9 15.0 %copy-start.28 = (f32[400]{0:T(512)S(1)}, f32[400]{0:T(512)}, u32[]{:S(2)}) copy-start(f32[400]{0:T(512)} %param.31) | copy-start | bytes 4804
  56.9 15.0 %copy-start.29 = (f32[53]{0:T(128)S(1)}, f32[53]{0:T(128)}, u32[]{:S(2)}) copy-start(f32[53]{0:T(128)} %param.34) | copy-start | bytes 640
  56.9 15.0 %copy-start.30 = (f32[53]{0:T(128)S(1)}, f32[53]{0:T(128)}, u32[]{:S(2)}) copy-start(f32[53]{0:T(128)} %param.33) | copy-start | bytes 640
  72.0 11.2 %copy-start.23 = (f32[53]{0:T(128)S(1)}, f32[53]{0:T(128)}, u32[]{:S(2)}) copy-start(f32[53]{0:T(128)} %param.35) | copy-start | bytes 640
  72.0 12.5 %copy-start.10 = (f32[8,8,256]{2,1,0:T(8,128)S(1)}, f32[8,8,256]{2,1,0:T(8,128)}, u32[]{:S(2)}) copy-start(f32[8,8,256]{2,1,0:T(8,128)} %abs_reduce_fusion) | copy-start | bytes 196612
  72.0 13.2 %copy-start.13 = (f32[1,8,8,255]{3,2,1,0:T(8,128)S(1)}, f32[1,8,8,255]{3,2,1,0:T(8,128)}, u32[]{:S(2)}) copy-start(f32[1,8,8,255]{3,2,1,0:T(8,128)} %get-tuple-element.37) | copy-start | bytes 195844
  72.0 13.2 %copy-start.14 = (f32[1,8,8,255]{3,2,1,0:T(8,128)S(1)}, f32[1,8,8,255]{3,2,1,0:T(8,128)}, u32[]{:S(2)}) copy-start(f32[1,8,8,255]{3,2,1,0:T(8,128)} %get-tuple-element.39) | copy-start | bytes 195844
  72.0 13.1 %copy-start.16 = (f32[1,8,8,1]{3,2,1,0:T(8,128)S(1)}, f32[1,8,8,1]{3,2,1,0:T(8,128)}, u32[]{:S(2)}) copy-start(f32[1,8,8,1]{3,2,1,0:T(8,128)} %get-tuple-element.41) | copy-start | bytes 772
  72.0 13.1 %copy-start.17 = (f32[1,8,8,1]{3,2,1,0:T(8,128)S(1)}, f32[1,8,8,1]{3,2,1,0:T(8,128)}, u32[]{:S(2)}) copy-start(f32[1,8,8,1]{3,2,1,0:T(8,128)} %get-tuple-element.42) | copy-start | bytes 772
  72.0 13.2 %copy-start.11 = (f32[8,8,255]{2,1,0:T(8,128)S(1)}, f32[8,8,255]{2,1,0:T(8,128)}, u32[]{:S(2)}) copy-start(f32[8,8,255]{2,1,0:T(8,128)} %get-tuple-element.36) | copy-start | bytes 195844
  72.0 13.2 %copy-start.12 = (f32[8,8,255]{2,1,0:T(8,128)S(1)}, f32[8,8,255]{2,1,0:T(8,128)}, u32[]{:S(2)}) copy-start(f32[8,8,255]{2,1,0:T(8,128)} %get-tuple-element.38) | copy-start | bytes 195844
  72.0 13.2 %copy-start.15 = (f32[8,8,1]{2,1,0:T(8,128)S(1)}, f32[8,8,1]{2,1,0:T(8,128)}, u32[]{:S(2)}) copy-start(f32[8,8,1]{2,1,0:T(8,128)} %get-tuple-element.43) | copy-start | bytes 772
  94.9 121.1 %collective-permute-start.3 = (f32[57,10,1,256]{3,2,1,0:T(1,128)}, f32[57,10,1,256]{3,2,1,0:T(1,128)S(1)}, u32[]{:S(2)}, u32[]{:S(2)}) collective-permute-start(f32[57,10,1,256]{3,2,1,0:T(1,128)} %get-tuple-element.19), channel_id=1, source_target_pairs={{0,1},{1,2},{2,3},{3,4},{4,5},{5,6},{6,7},{7,8},{8,9},{9,10},{10,1... | collective-permute-start | bytes 1751048 | tf_op jit(solution)/shard_map/ppermute | solution.py:12
  98.0 118.0 %collective-permute-start.2 = (f32[57,10,1,256]{3,2,1,0:T(1,128)}, f32[57,10,1,256]{3,2,1,0:T(1,128)S(1)}, u32[]{:S(2)}, u32[]{:S(2)}) collective-permute-start(f32[57,10,1,256]{3,2,1,0:T(1,128)} %get-tuple-element.18), channel_id=1, source_target_pairs={{1,0},{2,1},{3,2},{4,3},{5,4},{6,5},{7,6},{8,7},{9,8},{10,9},{11,1... | collective-permute-start | bytes 1751048 | tf_op jit(solution)/shard_map/ppermute | solution.py:15
  219.1 15.2 %copy-start.1 = (bf16[1600,800]{0,1:T(8,128)(2,1)S(1)}, bf16[1600,800]{0,1:T(8,128)(2,1)}, u32[]{:S(2)}) copy-start(bf16[1600,800]{0,1:T(8,128)(2,1)} %param.28) | copy-start | bytes 7680004
  (13 other events, 69.3 us)
where the time goes:
time: 235 us; the launch traced here: 234 us
  blocking collectives  72.8 us (31%)
  other arithmetic  63.7 us (27%)
  local copies, waits for them, and re-layouts  44.7 us (19%)
  matrix products  38.7 us (16%)
  starting transfers between devices  11.3 us (5%)
  between operations  3.17 us (1%)
    pmax x1, blocking collectives, shards(): lax.pmax(jnp.max(jnp.sum(jnp.abs(fluid_motion_vector), axis=0)), ('gx', '...  72.8 us
    scatter-add x1, other arithmetic, shards(): jnp.zeros((nspec + 1, ncells), jnp.float32).at[:, index].add(result.T)  26.4 us
    gather x1, local copies, waits for them, and re-layouts, shards(): inputs = normalize(jnp.take(fluid_snapshot, index, axis=1).T)  17.6 us
    dot_general x1, matrix products, chemistry(): jnp.dot(hidden, secondary_matrix, preferred_element_type=jnp.float32)  15 us
    add x1, other arithmetic, shards(): final = moved + change.reshape(nspec + 1, depth_x, depth_y, depth_z)  12.5 us
    dot_general x1, matrix products, chemistry(): jnp.dot(inputs, opening_matrix, preferred_element_type=jnp.float32)  12 us
    dot_general x1, matrix products, chemistry(): jnp.dot(hidden, closing_matrix, preferred_element_type=jnp.float32)  11.1 us
    concatenate x3, other arithmetic, shards(): jnp.concatenate([mixture_fractions, thermal_kelvins[None], fluid_motion_v...  10.9 us
  transfers between devices with their start and end apart: 4, of which 0 were waited for; matrix products, arithmetic and copies ran while one was open for 53% of the time, Pallas kernels for 0%

commit v1 on v0

v1 whole, which is shorter than its diff:
```python
import functools
import math

import jax
import jax.numpy as jnp
from jax import lax
from jax.experimental import pallas as pl
from jax.experimental.pallas import tpu as pltpu
from jax.sharding import PartitionSpec as P

f32 = jnp.float32
bf = jnp.bfloat16
i32 = jnp.int32
G = 8
U = 4
C = math.sqrt(2 / math.pi)
MESH = pl.DeviceIdType.MESH


def lane_gather(x, idx):
    return jnp.take_along_axis(x, idx, axis=1, mode="promise_in_bounds")


def prep_kernel(tally, listing, mix, temp, press, vel,
                packed, pos, offs, vmax, xs, ys,
                buf, velbuf, perm_ref, offs_smem, sems, osem):
    copies=[]
    for j in range(2):
        copies.append(pltpu.make_async_copy(mix.at[:, :, :, pl.ds(128*j,128)], buf.at[j, pl.ds(0,53)], sems.at[j]))
        copies.append(pltpu.make_async_copy(temp.at[:, :, pl.ds(128*j,128)], buf.at[j, 53], sems.at[2+j]))
        copies.append(pltpu.make_async_copy(press.at[:, :, pl.ds(128*j,128)], buf.at[j, 54], sems.at[4+j]))
    vc=pltpu.make_async_copy(vel, velbuf, sems.at[6])
    for c in copies: c.start()
    vc.start()
    buf[0,55]=jnp.zeros((8,8,128),f32); buf[1,55]=jnp.zeros((8,8,128),f32)
    n=tally[0,0]
    cells=listing[0]
    slot=lax.broadcasted_iota(i32,(1,4096),1)
    hi=jnp.where(slot<n, cells>>7, -1)
    lo=cells&127
    rows=lax.broadcasted_iota(i32,(128,4096),0)
    a=jnp.where(hi==rows,1.0,0.0).astype(bf)
    b=jnp.where(lo==rows,1.0,0.0).astype(bf)
    nt=(((1,),(1,)),((),()))
    mask=lax.dot_general(a,b,nt,preferred_element_type=f32)
    maskb=mask.astype(bf)
    ri=lax.broadcasted_iota(i32,(128,128),0); ci=lax.broadcasted_iota(i32,(128,128),1)
    incl=jnp.dot(maskb,jnp.where(ri<=ci,1.0,0.0).astype(bf),preferred_element_type=f32)
    cnt=jnp.dot(maskb,jnp.ones((128,128),bf),preferred_element_type=f32)
    off=jnp.dot(jnp.where(ci<ri,1.0,0.0).astype(bf),cnt.astype(bf),preferred_element_type=f32)
    cntr=lax.dot_general(jnp.ones((8,128),bf),maskb,nt,preferred_element_type=f32)
    up=jnp.where(lax.broadcasted_iota(i32,(128,256),0)<lax.broadcasted_iota(i32,(128,256),1),1.0,0.0).astype(bf)
    offr=jnp.dot(cntr.astype(bf),up,preferred_element_type=f32)
    offs[...]=offr.astype(i32)
    oc=pltpu.make_async_copy(offs, offs_smem, osem)
    oc.start()
    pos[...]=jnp.where(mask>0.5,(off+incl).astype(i32)-1,-1)
    want=(((ci-off.astype(i32))&127)+1).astype(f32)
    at=jnp.zeros((128,128),i32)
    for s in (64,32,16,8,4,2,1):
        v=lane_gather(incl,at+(s-1))
        at=jnp.where(v<want,at+s,at)
    perm_ref[...]=at
    oc.wait()
    vc.wait()
    s=jnp.abs(velbuf[0])+jnp.abs(velbuf[1])+jnp.abs(velbuf[2])
    s=jnp.max(s,axis=0)
    vmax[...]=jnp.maximum(s[:,:128],s[:,128:])
    for c in copies: c.wait()
    flat=buf.reshape(2*56*64,128)
    lane=lax.broadcasted_iota(i32,(56,128),1)
    def group(i,cur):
        gs=[]
        for k in range(G):
            r=i*G+k
            g=flat[pl.ds((k&1)*3584+i*(G//2)+(k>>1),56,stride=64),:]
            gs.append(lane_gather(g,jnp.broadcast_to(perm_ref[pl.ds(r,1),:],(56,128))))
        for k in range(G):
            r=i*G+k
            o=offs_smem[0,r]
            nx=offs_smem[0,r+1]
            t=o>>7
            cur=jnp.where(lane>=(o&127),gs[k],cur)
            packed[t]=cur
            cur=jnp.where((nx>>7)!=t,gs[k],cur)
        return cur
    cur=lax.fori_loop(0,128//G,group,jnp.zeros((56,128),f32),unroll=U)
    packed[n>>7]=cur
    for k,x in enumerate((0,7)):
        for j in range(2):
            xs[k,:54,:,128*j:128*j+128]=buf[j,:54,x]
            xs[k,54,:,128*j:128*j+128]=velbuf[0,x,:,128*j:128*j+128]
    for k,y in enumerate((0,7)):
        for j in range(2):
            ys[k,:54,:,128*j:128*j+128]=flat[pl.ds(j*3584+y,54*8,stride=8),:].reshape(54,8,128)
            ys[k,54,:,128*j:128*j+128]=velbuf[1,:,y,128*j:128*j+128]

def prep(tally,listing,mix,temp,press,vel):
    V=pl.BlockSpec(memory_space=pltpu.VMEM); A=pl.BlockSpec(memory_space=pl.ANY); S=pl.BlockSpec(memory_space=pltpu.SMEM)
    sd=jax.ShapeDtypeStruct
    return pl.pallas_call(prep_kernel,
        out_shape=(sd((33,56,128),f32),sd((128,128),i32),sd((8,256),i32),sd((8,128),f32),sd((2,55,8,256),f32),sd((2,55,8,256),f32)),
        in_specs=[S,V,A,A,A,A],out_specs=[V]*6,
        scratch_shapes=[pltpu.VMEM((2,56,8,8,128),f32),pltpu.VMEM((3,8,8,256),f32),pltpu.VMEM((128,128),i32),pltpu.SMEM((8,256),i32),pltpu.SemaphoreType.DMA((7,)),pltpu.SemaphoreType.DMA],
        compiler_params=pltpu.CompilerParams(vmem_limit_bytes=48<<20),name="prep")(tally,listing,mix,temp,press,vel)


NT = 8


def act(y, s):
    y2 = y * y
    u = y * ((C * 0.044715 / s**3) * y2 + (C / s))
    return (y + y * jnp.tanh(u)).astype(bf)


def col(row, n):
    return jnp.transpose(jnp.broadcast_to(row, (128, n)))


def wide(b, n):
    return jnp.concatenate([b] * (n // 128), axis=1)


def chem_kernel(packed, vmax, xs, ys, w1, b1, w2t, b2, w3t, b3, w4t, b4, inc, hr,
                out, gm, hx, hy,
                w1t, c2, c3, c4, s1, s2, m1, ssem1, rsem1, ssem2, rsem2, hsend, hrecv, *, nx, ny):
    gx, yz = lax.axis_index("gx"), lax.axis_index("yz")
    xpart = [(lax.rem(gx + k, nx), yz) for k in range(1, nx)]
    ypart = [(gx, lax.rem(yz + k, ny)) for k in range(1, ny)]
    barrier = pltpu.get_barrier_semaphore()
    for dev in xpart + ypart:
        pl.semaphore_signal(barrier, inc=1, device_id=dev, device_id_type=MESH)

    b = b1[...].reshape(1, 1600)
    hi = b.astype(bf).astype(f32)
    mid = (b - hi).astype(bf).astype(f32)
    lo = b - hi - mid
    wp = jnp.concatenate([w1[...].astype(f32), hi, mid, lo, jnp.zeros((70, 1600), f32)], axis=0)
    w1t[...] = jnp.transpose(wp)[:, :64].astype(bf)
    c2[...] = col(2.0 * b2[...].reshape(1, 800), 800)
    c3[...] = col(4.0 * b3[...].reshape(1, 400), 400)
    z = jnp.zeros((1, 3), f32)
    c4[0] = col(jnp.concatenate([8.0 * b4[...].reshape(1, 53), z], 1), 56)
    c4[1] = col(jnp.concatenate([inc[...].reshape(1, 53) * 0.125, z], 1), 56)
    c4[2] = col(jnp.concatenate([-hr[...].reshape(1, 53), z], 1), 56)
    n = NT * 128
    r = lax.broadcasted_iota(i32, (56, 1), 0)
    ce = jnp.where(r < 53, 0.1, jnp.where(r == 53, 1350.0, 1.0)).astype(f32)
    sp = jnp.where(r < 53, 0.06, jnp.where(r == 53, 600.0, 0.1)).astype(f32)
    tail = jnp.where(lax.broadcasted_iota(i32, (8, n), 0) < 2, 1.0, 0.0).astype(f32)
    rr = lax.broadcasted_iota(i32, (56, n), 0)

    def block(i, c):
        x = jnp.concatenate([packed[NT * i + k] for k in range(NT)], axis=1)
        x = jnp.where(r < 55, (x - ce) / sp, 1.0)
        x = jnp.concatenate([x, tail], axis=0).astype(bf)
        h = act(jnp.dot(w1t[...], x, preferred_element_type=f32), 1.0)
        a = jnp.dot(w2t[...], h, preferred_element_type=f32) + wide(c2[...], n)
        h = act(a, 2.0)
        a = jnp.dot(w3t[...], h, preferred_element_type=f32) + wide(c3[...], n)
        h = act(a, 4.0)
        a = jnp.dot(w4t[...], h, preferred_element_type=f32)
        a = jnp.concatenate([a, jnp.zeros((3, n), f32)], axis=0)
        d = (a + wide(c4[0], n)) * wide(c4[1], n)
        heat = jnp.sum(d * wide(c4[2], n), axis=0, keepdims=True)
        d = jnp.where(rr == 53, heat, d)
        for k in range(NT):
            out[NT * i + k] = d[:, k * 128:(k + 1) * 128]
        return c

    up_x, down_x = xpart[0], xpart[nx - 2]
    up_y, down_y = ypart[0], ypart[ny - 2]
    remote = lambda src, dst, a, b, dev: pltpu.make_async_remote_copy(
        src_ref=src, dst_ref=dst, send_sem=a, recv_sem=b, device_id=dev, device_id_type=MESH)
    halos = [remote(ys.at[1], hy.at[0], hsend.at[0], hrecv.at[0], up_y),
             remote(ys.at[0], hy.at[1], hsend.at[1], hrecv.at[1], down_y),
             remote(xs.at[1], hx.at[0], hsend.at[2], hrecv.at[2], up_x),
             remote(xs.at[0], hx.at[1], hsend.at[3], hrecv.at[3], down_x)]
    first = [remote(vmax, s1.at[k], ssem1.at[k], rsem1.at[k], ypart[k]) for k in range(ny - 1)]
    second = [remote(m1, s2.at[k], ssem2.at[k], rsem2.at[k], xpart[k]) for k in range(nx - 1)]

    nb = 32 // NT
    def step(i, c):
        @pl.when(i == 0)
        def _():
            pl.semaphore_wait(barrier, nx + ny - 2)
            for cp in first + halos:
                cp.start()

        @pl.when(i == 1)
        def _():
            for cp in first:
                cp.wait()
            m1[...] = jnp.maximum(vmax[...], jnp.max(s1[...], axis=0))
            for cp in second:
                cp.start()

        @pl.when(i == nb - 1)
        def _():
            for cp in second:
                cp.wait()
            gm[...] = jnp.maximum(m1[...], jnp.max(s2[...], axis=0))

        return block(i, c)

    lax.fori_loop(0, nb, step, 0)
    for cp in halos:
        cp.wait()


def chem(nx, ny, packed, vmax, xs, ys, w1, b1, w2, b2, w3, b3, w4, b4, inc, hr):
    V = pl.BlockSpec(memory_space=pltpu.VMEM)
    A = pl.BlockSpec(memory_space=pl.ANY)
    sd = jax.ShapeDtypeStruct
    sem = pltpu.SemaphoreType.DMA
    return pl.pallas_call(
        functools.partial(chem_kernel, nx=nx, ny=ny),
        out_shape=(sd((33, 56, 128), f32), sd((8, 128), f32), sd((2, 55, 8, 256), f32), sd((2, 55, 8, 256), f32)),
        in_specs=[V, V, A, A] + [V] * 10,
        out_specs=[V, V, A, A],
        scratch_shapes=[
            pltpu.VMEM((1600, 64), bf), pltpu.VMEM((800, 128), f32), pltpu.VMEM((400, 128), f32),
            pltpu.VMEM((3, 56, 128), f32),
            pltpu.VMEM((ny - 1, 8, 128), f32), pltpu.VMEM((nx - 1, 8, 128), f32), pltpu.VMEM((8, 128), f32),
            sem((ny - 1,)), sem((ny - 1,)), sem((nx - 1,)), sem((nx - 1,)), sem((4,)), sem((4,)),
        ],
        compiler_params=pltpu.CompilerParams(vmem_limit_bytes=48 << 20, collective_id=0, has_side_effects=True),
        name="chem",
    )(packed, vmax, xs, ys, w1, b1, w2.T, b2, w3.T, b3, w4.T, b4, inc, hr)


def edges(nx, ny):
    gx, yz = lax.axis_index("gx"), lax.axis_index("yz")
    flag = lambda c: jnp.where(c, 1.0, 0.0).astype(f32)
    return flag(gx > 0), flag(gx < nx - 1), flag(yz > 0), flag(yz < ny - 1)


FB=8
def finish_kernel(offs, kappa, gm, pos, d, hx, hy, vel, temp, mix, out, tout, coef, ebuf, dtv, *, edges):
    step=pl.program_id(0)
    flat=ebuf.reshape(2*56*64,128)
    lo_x,hi_x,lo_y,hi_y=edges()
    @pl.when(step==0)
    def _():
        kmax=lax.fori_loop(1,54,lambda k,c: jnp.maximum(c,kappa[k]),kappa[0])
        m=jnp.max(gm[...])
        dt=0.9/(jnp.full((8,256),m)+6.0*kmax)
        dtv[...]=dt
        rows=lax.broadcasted_iota(i32,(8,256),0)
        for x in range(8):
            u0=vel[0,x]; u1=vel[1,x]; u2=vel[2,x]
            xp=vel[0,x+1] if x<7 else hx[1,54]*hi_x
            xm=vel[0,x-1] if x>0 else hx[0,54]*lo_x
            yp=jnp.where(rows==7,hy[1,54,x:x+1,:]*hi_y,pltpu.roll(u1,7,0))
            ym=jnp.where(rows==0,hy[0,54,x:x+1,:]*lo_y,pltpu.roll(u1,1,0))
            zp=pltpu.roll(u2,255,1); zm=pltpu.roll(u2,1,1)
            h=0.5*dt
            c0=jnp.ones((8,256),f32)
            for k,(u,p,q) in enumerate(((u0,xp,xm),(u1,yp,ym),(u2,zp,zm))):
                wp=h*(u+p); wm=h*(q+u)
                coef[2*k,x]=-jnp.minimum(wp,0.0)
                coef[2*k+1,x]=jnp.maximum(wm,0.0)
                c0=c0-(jnp.maximum(wp,0.0)-jnp.minimum(wm,0.0))
            coef[6,x]=c0
        lane=lax.broadcasted_iota(i32,(56,128),1)
        G=8
        def group(i,c):
            gs=[]
            for k in range(G):
                r=i*G+k
                o=offs[0,r]
                t=o>>7
                m=jnp.where(lane>=(o&127),d[t],d[jnp.minimum(t+1,32)])
                p=jnp.broadcast_to(pos[pl.ds(r,1),:],(56,128))
                g=lane_gather(m,p&127)
                gs.append(jnp.where(p>=0,g,0.0))
            for k in range(G):
                flat[pl.ds((k&1)*3584+i*(G//2)+(k>>1),56,stride=64),:]=gs[k]
            return c
        lax.fori_loop(0,128//G,group,0,unroll=2)
    rows=lax.broadcasted_iota(i32,(8,256),0)
    def field(f, load, store):
        kd=kappa[f]*dtv[...]
        hyl=hy[0,f]*lo_y; hyh=hy[1,f]*hi_y
        c6=6.0*kd
        for x in range(8):
            v=load(x)
            xp=load(x+1) if x<7 else hx[1,f]*hi_x
            xm=load(x-1) if x>0 else hx[0,f]*lo_x
            yp=jnp.where(rows==7,hyh[x:x+1,:],pltpu.roll(v,7,0))
            ym=jnp.where(rows==0,hyl[x:x+1,:],pltpu.roll(v,1,0))
            zp=pltpu.roll(v,255,1); zm=pltpu.roll(v,1,1)
            acc=(coef[6,x]-c6)*v
            for k,n in enumerate((xp,xm,yp,ym,zp,zm)):
                acc=acc+(coef[k,x]+kd)*n
            e=jnp.concatenate([ebuf[0,f,x],ebuf[1,f,x]],axis=1)
            store(x,acc+e)
    def loop(i,c):
        def st(x,v): out[i,x]=v
        field(step*FB+i,lambda x: mix[i,x],st)
        return c
    @pl.when(step<6)
    def _():
        lax.fori_loop(0,FB,loop,0)
    @pl.when(step==6)
    def _():
        lax.fori_loop(0,5,loop,0)
        def st(x,v): tout[x]=v
        field(53,lambda x: temp[x],st)

def finish(edges,offs,kappa,gm,pos,d,hx,hy,vel,temp,mix):
    V=pl.BlockSpec(memory_space=pltpu.VMEM); S=pl.BlockSpec(memory_space=pltpu.SMEM)
    sd=jax.ShapeDtypeStruct
    full=lambda a: pl.BlockSpec(a.shape,lambda i,n=a.ndim:(0,)*n)
    blk=pl.BlockSpec((FB,8,8,256),lambda i:(i,0,0,0))
    return pl.pallas_call(functools.partial(finish_kernel,edges=edges),
        grid=(7,),
        out_shape=(sd((53,8,8,256),f32),sd((8,8,256),f32)),
        in_specs=[S,S]+[V]*7+[blk],out_specs=[blk,pl.BlockSpec((8,8,256),lambda i:(0,0,0))],
        scratch_shapes=[pltpu.VMEM((7,8,8,256),f32),pltpu.VMEM((2,56,8,8,128),f32),pltpu.VMEM((8,256),f32)],
        compiler_params=pltpu.CompilerParams(vmem_limit_bytes=48<<20),name="finish")(offs,kappa,gm,pos,d,hx,hy,vel,temp,mix)


def shards(nx, ny, mix, temp, press, vel, kappa, tally, listing, *weights):
    packed, pos, offs, vmax, xs, ys = prep(tally, listing, mix, temp, press, vel)
    d, gm, hx, hy = chem(nx, ny, packed, vmax, xs, ys, *weights)
    return finish(functools.partial(edges, nx, ny), offs, kappa, gm, pos, d, hx, hy, vel, temp, mix)


def solution(mesh):
    in_specs = (
        P(None, "gx", "yz", None),
        P("gx", "yz", None),
        P("gx", "yz", None),
        P(None, "gx", "yz", None),
        P(),
        P("gx", "yz"),
        P("gx", "yz", None),
    ) + (P(),) * 10
    out_specs = (P(None, "gx", "yz", None), P("gx", "yz", None))
    nx, ny = mesh.shape["gx"], mesh.shape["yz"]
    return jax.shard_map(functools.partial(shards, nx, ny), mesh=mesh, in_specs=in_specs, out_specs=out_specs, check_vma=False)
```

time: 235 us -> 62 us (0.26)
  the two profiles are of different devices: /device:TPU:1 before, /device:TPU:14 now
where the time goes in v1:
time: 62 us; the launch traced here: 61.5 us
  Pallas kernels  55.8 us (90%)
  local copies, waits for them, and re-layouts  4.29 us (7%)
  between operations  1.49 us (2%)
    pallas_call x1, Pallas kernels, chem(): pl.pallas_call(functools.partial(chem_kernel, nx=nx, ny=ny), out_shape=(s...  36.8 us
    pallas_call x1, Pallas kernels, finish(): pl.pallas_call(functools.partial(finish_kernel, edges=edges), grid=(7,),...  13.4 us
    pallas_call x1, Pallas kernels, prep(): pl.pallas_call(prep_kernel, out_shape=(sd((33, 56, 128), f32), sd((128, 1...  5.49 us
    unnamed x34, local copies, waits for them, and re-layouts  4.29 us

profile of v1, /device:TPU:14, one launch (start us, length us, event | category | flops | bytes accessed | tf_op | source)
XLA Modules:
  0.0 61.5 jit_solution(15533510570073706036)
XLA Ops:
  0.6 0.0 copy-start.15
  0.6 0.0 copy-start.14
  0.7 0.0 copy-start.13
  0.7 0.0 copy-start.12
  0.7 0.0 copy-start.11
  1.4 0.0 copy-start.1
  1.4 0.9 %copy-done.1 = f32[3,8,8,256]{3,2,1,0:T(8,128)S(1)} copy-done((f32[3,8,8,256]{3,2,1,0:T(8,128)S(1)}, f32[3,8,8,256]{3,2,1,0:T(8,128)}, u32[]{:S(2)}) %copy-start.1) | copy-done | bytes 196632
  2.3 0.8 %copy-done.4 = f32[8,8,256]{2,1,0:T(8,128)S(1)} copy-done((f32[8,8,256]{2,1,0:T(8,128)S(1)}, f32[8,8,256]{2,1,0:T(8,128)}, u32[]{:S(2)}) %copy-start.4) | copy-done | bytes 65560
  3.1 0.8 %copy-done.7 = f32[8,8,256]{2,1,0:T(8,128)S(1)} copy-done((f32[8,8,256]{2,1,0:T(8,128)S(1)}, f32[8,8,256]{2,1,0:T(8,128)}, u32[]{:S(2)}) %copy-start.7) | copy-done | bytes 65560
  4.0 0.7 %copy-done.9 = s32[1,1,4096]{2,1,0:T(1,128)S(1)} copy-done((s32[1,1,4096]{2,1,0:T(1,128)S(1)}, s32[1,1,4096]{2,1,0:T(1,128)}, u32[]{:S(2)}) %copy-start.9) | copy-done | bytes 16408
  4.7 5.5 %prep.1 = (f32[33,56,128]{2,1,0:T(8,128)S(1)}, s32[128,128]{1,0:T(8,128)S(1)}, s32[8,256]{1,0:T(8,128)S(1)}, f32[8,128]{1,0:T(8,128)S(1)}, f32[2,55,8,256]{3,2,1,0:T(8,128)S(1)}, /*index=5*/f32[2,55,8,256]{3,2,1,0:T(8,128)S(1)}) custom-call(s32[1,1]{1,0:T(1,128)S(6)} %copy.19.tally, s32[1,1,4096]{2,1,0:T(1,128)S(1)} %copy-done.9, f32[53,8,8,256]{3,2,1,0:T(8,128)} %mix.3, ...), custom_call_target="tpu_custom_call" | custom-call | tf_op jit(solution)/shard_map/prep/pallas_call | solution.py:101
  10.2 0.0 copy-start
  10.2 0.9 %copy-done = f32[33,56,128]{2,1,0:T(8,128)} copy-done((f32[33,56,128]{2,1,0:T(8,128)}, f32[33,56,128]{2,1,0:T(8,128)S(1)}, u32[]{:S(2)}) %copy-start) | copy-done | bytes 946200
  11.1 0.0 copy-done.15
  11.2 0.0 copy-done.14
  11.2 0.0 copy-done.13
  11.2 0.0 copy-done.12
  11.2 0.0 copy-done.11
  11.2 0.0 copy-done.3
  11.2 0.0 copy-done.6
  11.2 0.0 copy-done.8
  11.2 0.0 copy-done.10
  11.2 36.8 %chem.1 = (f32[33,56,128]{2,1,0:T(8,128)S(1)}, f32[8,128]{1,0:T(8,128)S(1)}, f32[2,55,8,256]{3,2,1,0:T(8,128)S(1)}, f32[2,55,8,256]{3,2,1,0:T(8,128)S(1)}) custom-call(f32[33,56,128]{2,1,0:T(8,128)} %copy-done, f32[8,128]{1,0:T(8,128)S(1)} %get-tuple-element.14.vmax, f32[2,55,8,256]{3,2,1,0:T(8,128)S(1)} %get-tuple-element.15.xs, ...), custom_call_target="tpu_custom_call" | custom-call | tf_op jit(solution)/shard_map/chem/pallas_call | solution.py:217
  48.1 13.4 %finish.1 = (f32[53,8,8,256]{3,2,1,0:T(8,128)}, f32[8,8,256]{2,1,0:T(8,128)}) custom-call(s32[8,256]{1,0:T(8,128)S(1)} %get-tuple-element.12.offs, f32[54]{0:T(128)S(1)} %copy-done.16, f32[8,128]{1,0:T(8,128)S(1)} %get-tuple-element.17.gm, s32[128,128]{1,0:T(8,128)S(1)} %get-tuple-element.18.pos, f32[33,56,128]{2,1,0:T(8,128)S(1)} %get-tuple-element.19.d, ...), custom_call_target="tpu_custom_call" | custom-call | tf_op jit(solution)/shard_map/finish/pallas_call | solution.py:317
  (13 shorter events, 0.0 us)
Async XLA Ops:
  0.6 10.5 %copy-start.15 = (f32[53]{0:T(128)S(1)}, f32[53]{0:T(128)}, u32[]{:S(2)}) copy-start(f32[53]{0:T(128)} %hr.1) | copy-start | bytes 640
  0.6 10.5 %copy-start.14 = (f32[53]{0:T(128)S(1)}, f32[53]{0:T(128)}, u32[]{:S(2)}) copy-start(f32[53]{0:T(128)} %inc.1) | copy-start | bytes 640
  0.7 10.5 %copy-start.13 = (f32[53]{0:T(128)S(1)}, f32[53]{0:T(128)}, u32[]{:S(2)}) copy-start(f32[53]{0:T(128)} %b4.1) | copy-start | bytes 640
  0.7 10.5 %copy-start.12 = (f32[400]{0:T(512)S(1)}, f32[400]{0:T(512)}, u32[]{:S(2)}) copy-start(f32[400]{0:T(512)} %b3.1) | copy-start | bytes 4804
  0.7 10.5 %copy-start.11 = (f32[800]{0:T(1024)S(1)}, f32[800]{0:T(1024)}, u32[]{:S(2)}) copy-start(f32[800]{0:T(1024)} %b2.1) | copy-start | bytes 9604
  1.4 0.9 %copy-start.1 = (f32[3,8,8,256]{3,2,1,0:T(8,128)S(1)}, f32[3,8,8,256]{3,2,1,0:T(8,128)}, u32[]{:S(2)}) copy-start(f32[3,8,8,256]{3,2,1,0:T(8,128)} %vel.3) | copy-start | bytes 589828
  2.3 0.8 %copy-start.4 = (f32[8,8,256]{2,1,0:T(8,128)S(1)}, f32[8,8,256]{2,1,0:T(8,128)}, u32[]{:S(2)}) copy-start(f32[8,8,256]{2,1,0:T(8,128)} %temp.3) | copy-start | bytes 196612
  3.1 0.8 %copy-start.7 = (f32[8,8,256]{2,1,0:T(8,128)S(1)}, f32[8,8,256]{2,1,0:T(8,128)}, u32[]{:S(2)}) copy-start(f32[8,8,256]{2,1,0:T(8,128)} %press.1) | copy-start | bytes 196612
  4.0 0.7 %copy-start.9 = (s32[1,1,4096]{2,1,0:T(1,128)S(1)}, s32[1,1,4096]{2,1,0:T(1,128)}, u32[]{:S(2)}) copy-start(s32[1,1,4096]{2,1,0:T(1,128)} %listing.1) | copy-start | bytes 49156
  4.7 6.5 %copy-start.3 = (bf16[800,400]{0,1:T(8,128)(2,1)S(1)}, bf16[800,400]{0,1:T(8,128)(2,1)}, u32[]{:S(2)}) copy-start(bf16[800,400]{0,1:T(8,128)(2,1)} %param.28) | copy-start | bytes 1920004
  4.7 6.5 %copy-start.6 = (bf16[55,1600]{1,0:T(8,128)(2,1)S(1)}, bf16[55,1600]{1,0:T(8,128)(2,1)}, u32[]{:S(2)}) copy-start(bf16[55,1600]{1,0:T(8,128)(2,1)} %w1.1) | copy-start | bytes 528004
  4.7 6.5 %copy-start.8 = (bf16[400,53]{0,1:T(8,128)(2,1)S(1)}, bf16[400,53]{0,1:T(8,128)(2,1)}, u32[]{:S(2)}) copy-start(bf16[400,53]{0,1:T(8,128)(2,1)} %param.30) | copy-start | bytes 127204
  4.7 6.5 %copy-start.10 = (f32[1600]{0:T(1024)S(1)}, f32[1600]{0:T(1024)}, u32[]{:S(2)}) copy-start(f32[1600]{0:T(1024)} %b1.1) | copy-start | bytes 19204
  10.2 0.9 %copy-start = (f32[33,56,128]{2,1,0:T(8,128)}, f32[33,56,128]{2,1,0:T(8,128)S(1)}, u32[]{:S(2)}) copy-start(f32[33,56,128]{2,1,0:T(8,128)S(1)} %get-tuple-element.13.packed) | copy-start | bytes 2838532
  11.1 36.9 %copy-start.2 = (f32[3,8,8,256]{3,2,1,0:T(8,128)S(1)}, f32[3,8,8,256]{3,2,1,0:T(8,128)}, u32[]{:S(2)}) copy-start(f32[3,8,8,256]{3,2,1,0:T(8,128)} %vel.3) | copy-start | bytes 589828
  11.1 36.9 %copy-start.5 = (f32[8,8,256]{2,1,0:T(8,128)S(1)}, f32[8,8,256]{2,1,0:T(8,128)}, u32[]{:S(2)}) copy-start(f32[8,8,256]{2,1,0:T(8,128)} %temp.3) | copy-start | bytes 196612
  11.1 36.9 %copy-start.16 = (f32[54]{0:T(128)S(1)}, f32[54]{0:T(128)}, u32[]{:S(2)}) copy-start(f32[54]{0:T(128)} %kappa.1) | copy-start | bytes 652

commit v2 on v1

v2 whole, which is shorter than its diff:
```python
import functools
import math

import jax
import jax.numpy as jnp
from jax import lax
from jax.experimental import pallas as pl
from jax.experimental.pallas import tpu as pltpu
from jax.sharding import PartitionSpec as P

f32 = jnp.float32
bf = jnp.bfloat16
i32 = jnp.int32
C = math.sqrt(2 / math.pi)
MESH = pl.DeviceIdType.MESH
VMEM = pl.BlockSpec(memory_space=pltpu.VMEM)
SMEM = pl.BlockSpec(memory_space=pltpu.SMEM)
HBM = pl.BlockSpec(memory_space=pltpu.HBM)
sd = jax.ShapeDtypeStruct
dma = pltpu.SemaphoreType.DMA
G = 8
NT = 8
PITCH = 72
HALF = 56 * PITCH


def lane_gather(x, idx):
    return jnp.take_along_axis(x, idx, axis=1, mode="promise_in_bounds")


def groups(x):
    return [x[8 * k:8 * k + 8] for k in range(7)]


def start_row(i, k):
    return (k & 1) * HALF + i * (G // 2) + (k >> 1)


def prep_kernel(tally, listing, mix, temp, press, vel,
                packed, pos, offs, vmax, xs, ys,
                buf, velbuf, lst, perm_ref, offs_smem, sems, lsem, osem):
    lc = pltpu.make_async_copy(listing.at[0], lst, lsem)
    lc.start()
    copies = [pltpu.make_async_copy(vel, velbuf, sems.at[6])]
    for j in range(2):
        lanes = pl.ds(128 * j, 128)
        copies.append(pltpu.make_async_copy(mix.at[:, :, :, lanes], buf.at[j, pl.ds(0, 53), pl.ds(0, 8)], sems.at[j]))
        copies.append(pltpu.make_async_copy(temp.at[:, :, lanes], buf.at[j, 53, pl.ds(0, 8)], sems.at[2 + j]))
        copies.append(pltpu.make_async_copy(press.at[:, :, lanes], buf.at[j, 54, pl.ds(0, 8)], sems.at[4 + j]))
    for c in copies:
        c.start()
    buf[0, 55] = jnp.zeros((9, 8, 128), f32)
    buf[1, 55] = jnp.zeros((9, 8, 128), f32)
    n = tally[0, 0]
    lc.wait()
    cells = lst[...]
    slot = lax.broadcasted_iota(i32, (1, 4096), 1)
    hi = jnp.where(slot < n, cells >> 7, -1)
    lo = cells & 127
    rows = lax.broadcasted_iota(i32, (128, 4096), 0)
    a = jnp.where(hi == rows, 1.0, 0.0).astype(bf)
    b = jnp.where(lo == rows, 1.0, 0.0).astype(bf)
    nt = (((1,), (1,)), ((), ()))
    mask = lax.dot_general(a, b, nt, preferred_element_type=f32)
    maskb = mask.astype(bf)
    ri = lax.broadcasted_iota(i32, (128, 128), 0)
    ci = lax.broadcasted_iota(i32, (128, 128), 1)
    before = lax.broadcasted_iota(i32, (128, 256), 0) < lax.broadcasted_iota(i32, (128, 256), 1)
    cntr = lax.dot_general(jnp.ones((8, 128), bf), maskb, nt, preferred_element_type=f32)
    offs[...] = jnp.dot(cntr.astype(bf), jnp.where(before, 1.0, 0.0).astype(bf), preferred_element_type=f32).astype(i32)
    oc = pltpu.make_async_copy(offs, offs_smem, osem)
    oc.start()
    incl = jnp.dot(maskb, jnp.where(ri <= ci, 1.0, 0.0).astype(bf), preferred_element_type=f32)
    cnt = jnp.dot(maskb, jnp.ones((128, 128), bf), preferred_element_type=f32)
    off = jnp.dot(jnp.where(ci < ri, 1.0, 0.0).astype(bf), cnt.astype(bf), preferred_element_type=f32)
    pos[...] = jnp.where(mask > 0.5, (off + incl).astype(i32) - 1, -1)
    want = (((ci - off.astype(i32)) & 127) + 1).astype(f32)
    at = jnp.zeros((128, 128), i32)
    for s in (64, 32, 16, 8, 4, 2, 1):
        v = lane_gather(incl, at + (s - 1))
        at = jnp.where(v < want, at + s, at)
    perm_ref[...] = at
    copies[0].wait()
    s = jnp.abs(velbuf[0]) + jnp.abs(velbuf[1]) + jnp.abs(velbuf[2])
    s = jnp.max(s, axis=0)
    vmax[...] = jnp.maximum(s[:, :128], s[:, 128:])
    for c in copies[1:]:
        c.wait()
    oc.wait()
    flat = buf.reshape(2 * HALF, 128)
    lane = lax.broadcasted_iota(i32, (8, 128), 1)

    def group(i, cur):
        gs = []
        for k in range(G):
            g = flat[pl.ds(start_row(i, k), 56, stride=PITCH), :]
            p = jnp.broadcast_to(perm_ref[pl.ds(i * G + k, 1), :], (8, 128))
            gs.append([lane_gather(x, p) for x in groups(g)])
        for k in range(G):
            o = offs_smem[0, i * G + k]
            t = o >> 7
            m = lane >= (o & 127)
            fresh = (offs_smem[0, i * G + k + 1] >> 7) != t
            cur = [jnp.where(m, g, c) for g, c in zip(gs[k], cur)]
            for q in range(7):
                packed[t, 8 * q:8 * q + 8] = cur[q]
            cur = [jnp.where(fresh, g, c) for g, c in zip(gs[k], cur)]
        return tuple(cur)

    cur = lax.fori_loop(0, 128 // G, group, tuple(jnp.zeros((8, 128), f32) for _ in range(7)), unroll=4)
    for q in range(7):
        packed[n >> 7, 8 * q:8 * q + 8] = cur[q]
    for k, x in enumerate((0, 7)):
        u = velbuf[0, x]
        uh = u.astype(bf).astype(f32)
        xs[k, 432:448] = jnp.concatenate([uh, u - uh], axis=0).astype(bf)
        for j in range(2):
            xs[k, 0:432, 128 * j:128 * j + 128] = buf[j, 0:54, x].reshape(432, 128).astype(bf)
    for k, y in enumerate((0, 7)):
        u = velbuf[1, :, y, :]
        uh = u.astype(bf).astype(f32)
        ys[k, 432:448] = jnp.concatenate([uh, u - uh], axis=0).astype(bf)
        for j in range(2):
            for f in range(0, 54, 2):
                z = [flat[pl.ds(j * HALF + (f + q) * PITCH + y, 8, stride=8), :] for q in range(2)]
                ys[k, 8 * f:8 * f + 16, 128 * j:128 * j + 128] = jnp.concatenate(z, axis=0).astype(bf)


def in_hbm(*arrays):
    return [pltpu.with_memory_space_constraint(a, pltpu.HBM) for a in arrays]


def prep(tally, listing, mix, temp, press, vel):
    return pl.pallas_call(
        prep_kernel,
        out_shape=(sd((33, 56, 128), f32), sd((128, 128), i32), sd((8, 256), i32), sd((8, 128), f32),
                   sd((2, 448, 256), bf), sd((2, 448, 256), bf)),
        in_specs=[SMEM] + [HBM] * 5,
        out_specs=[VMEM] * 6,
        scratch_shapes=[pltpu.VMEM((2, 56, 9, 8, 128), f32), pltpu.VMEM((3, 8, 8, 256), f32), pltpu.VMEM((1, 4096), i32),
                        pltpu.VMEM((128, 128), i32), pltpu.SMEM((8, 256), i32), dma((7,)), dma, dma],
        compiler_params=pltpu.CompilerParams(vmem_limit_bytes=20 << 20),
        name="prep",
    )(tally, *in_hbm(listing, mix, temp, press, vel))


def act(y, s):
    y2 = y * y
    u = y * ((C * 0.044715 / s**3) * y2 + (C / s))
    return (y + y * jnp.tanh(u)).astype(bf)


def col(row, n):
    return jnp.transpose(jnp.broadcast_to(row, (128, n)))


def wide(b, n):
    return jnp.concatenate([b] * (n // 128), axis=1)


def chem_kernel(packed, vmax, xs, ys, w1, b1, w2t, b2, w3t, b3, w4t, b4, inc, hr,
                out, gm, hx, hy,
                w1t, c2, c3, c4, s1, s2, m1, ssem1, rsem1, ssem2, rsem2, hsend, hrecv, *, nx, ny):
    gx, yz = lax.axis_index("gx"), lax.axis_index("yz")
    xpart = [(lax.rem(gx + k, nx), yz) for k in range(1, nx)]
    ypart = [(gx, lax.rem(yz + k, ny)) for k in range(1, ny)]
    barrier = pltpu.get_barrier_semaphore()
    for dev in xpart + ypart:
        pl.semaphore_signal(barrier, inc=1, device_id=dev, device_id_type=MESH)

    b = b1[...].reshape(1, 1600)
    hi = b.astype(bf).astype(f32)
    mid = (b - hi).astype(bf).astype(f32)
    lo = b - hi - mid
    wp = jnp.concatenate([w1[...].astype(f32), hi, mid, lo, jnp.zeros((70, 1600), f32)], axis=0)
    w1t[...] = jnp.transpose(wp)[:, :64].astype(bf)
    c2[...] = col(2.0 * b2[...].reshape(1, 800), 800)
    c3[...] = col(4.0 * b3[...].reshape(1, 400), 400)
    z = jnp.zeros((1, 3), f32)
    c4[0] = col(jnp.concatenate([8.0 * b4[...].reshape(1, 53), z], 1), 56)
    c4[1] = col(jnp.concatenate([inc[...].reshape(1, 53) * 0.125, z], 1), 56)
    c4[2] = col(jnp.concatenate([-hr[...].reshape(1, 53), z], 1), 56)
    n = NT * 128
    r = lax.broadcasted_iota(i32, (56, 1), 0)
    ce = jnp.where(r < 53, 0.1, jnp.where(r == 53, 1350.0, 1.0)).astype(f32)
    sp = jnp.where(r < 53, 0.06, jnp.where(r == 53, 600.0, 0.1)).astype(f32)
    tail = jnp.where(lax.broadcasted_iota(i32, (8, n), 0) < 2, 1.0, 0.0).astype(f32)
    rr = lax.broadcasted_iota(i32, (56, n), 0)

    up_x, down_x = xpart[0], xpart[nx - 2]
    up_y, down_y = ypart[0], ypart[ny - 2]
    remote = lambda src, dst, a, b, dev: pltpu.make_async_remote_copy(
        src_ref=src, dst_ref=dst, send_sem=a, recv_sem=b, device_id=dev, device_id_type=MESH)
    halos = [remote(ys.at[1], hy.at[0], hsend.at[0], hrecv.at[0], up_y),
             remote(ys.at[0], hy.at[1], hsend.at[1], hrecv.at[1], down_y),
             remote(xs.at[1], hx.at[0], hsend.at[2], hrecv.at[2], up_x),
             remote(xs.at[0], hx.at[1], hsend.at[3], hrecv.at[3], down_x)]
    first = [remote(vmax, s1.at[k], ssem1.at[k], rsem1.at[k], ypart[k]) for k in range(ny - 1)]
    second = [remote(m1, s2.at[k], ssem2.at[k], rsem2.at[k], xpart[k]) for k in range(nx - 1)]

    def exchange(i):
        @pl.when(i == 1)
        def _():
            pl.semaphore_wait(barrier, nx + ny - 2)
            for cp in first + halos:
                cp.start()

        @pl.when(i == 2)
        def _():
            for cp in first:
                cp.wait()
            m1[...] = jnp.maximum(vmax[...], jnp.max(s1[...], axis=0))
            for cp in second:
                cp.start()

    def block(i, c):
        x = jnp.concatenate([packed[NT * i + k] for k in range(NT)], axis=1)
        x = jnp.where(r < 55, (x - ce) / sp, 1.0)
        x = jnp.concatenate([x, tail], axis=0).astype(bf)
        h = act(jnp.dot(w1t[...], x, preferred_element_type=f32), 1.0)
        a = jnp.dot(w2t[...], h, preferred_element_type=f32) + wide(c2[...], n)
        h = act(a, 2.0)
        a = jnp.dot(w3t[...], h, preferred_element_type=f32) + wide(c3[...], n)
        h = act(a, 4.0)
        a = jnp.dot(w4t[...], h, preferred_element_type=f32)
        a = jnp.concatenate([a, jnp.zeros((3, n), f32)], axis=0)
        d = (a + wide(c4[0], n)) * wide(c4[1], n)
        heat = jnp.sum(d * wide(c4[2], n), axis=0, keepdims=True)
        d = jnp.where(rr == 53, heat, d)
        for k in range(NT):
            out[NT * i + k] = d[:, k * 128:(k + 1) * 128]
        exchange(i)
        return c

    lax.fori_loop(0, 32 // NT, block, 0)
    for cp in second:
        cp.wait()
    gm[...] = jnp.maximum(m1[...], jnp.max(s2[...], axis=0))
    for cp in halos:
        cp.wait()


def chem(nx, ny, packed, vmax, xs, ys, w1, b1, w2, b2, w3, b3, w4, b4, inc, hr):
    return pl.pallas_call(
        functools.partial(chem_kernel, nx=nx, ny=ny),
        out_shape=(sd((33, 56, 128), f32), sd((8, 128), f32), sd((2, 448, 256), bf), sd((2, 448, 256), bf)),
        in_specs=[VMEM] * 14,
        out_specs=[VMEM] * 4,
        scratch_shapes=[
            pltpu.VMEM((1600, 64), bf), pltpu.VMEM((800, 128), f32), pltpu.VMEM((400, 128), f32),
            pltpu.VMEM((3, 56, 128), f32),
            pltpu.VMEM((ny - 1, 8, 128), f32), pltpu.VMEM((nx - 1, 8, 128), f32), pltpu.VMEM((8, 128), f32),
            dma((ny - 1,)), dma((ny - 1,)), dma((nx - 1,)), dma((nx - 1,)), dma((4,)), dma((4,)),
        ],
        compiler_params=pltpu.CompilerParams(vmem_limit_bytes=32 << 20, collective_id=0, has_side_effects=True),
        name="chem",
    )(packed, vmax, xs, ys, w1, b1, w2.T, b2, w3.T, b3, w4.T, b4, inc, hr)


def finish_kernel(offs, kappa, kapv, gm, pos, d, hx, hy, vel, temp, mix, out, tout,
                  coef, ebuf, obuf, hxf, hyf, sems, *, edges):
    flat = ebuf.reshape(2 * HALF, 128)
    lo_x, hi_x, lo_y, hi_y = edges()
    rows = lax.broadcasted_iota(i32, (8, 256), 0)
    lane = lax.broadcasted_iota(i32, (8, 128), 1)
    for k, (fx, fy) in enumerate(((lo_x, lo_y), (hi_x, hi_y))):
        hxf[k] = (hx[k].astype(f32) * fx).reshape(56, 8, 256)
        hyf[k] = (hy[k].astype(f32) * fy).reshape(56, 8, 256)
    dt = 0.9 / (jnp.full((8, 256), jnp.max(gm[...])) + 6.0 * jnp.max(kapv[...].reshape(1, 54)))
    h = 0.5 * dt
    ux = [hxf[k, 54] + hxf[k, 55] for k in range(2)]
    uy = [hyf[k, 54] + hyf[k, 55] for k in range(2)]
    for x in range(8):
        u0 = vel[0, x]
        u1 = vel[1, x]
        u2 = vel[2, x]
        xp = vel[0, x + 1] if x < 7 else ux[1]
        xm = vel[0, x - 1] if x > 0 else ux[0]
        yp = jnp.where(rows == 7, uy[1][x:x + 1, :], pltpu.roll(u1, 7, 0))
        ym = jnp.where(rows == 0, uy[0][x:x + 1, :], pltpu.roll(u1, 1, 0))
        zp = pltpu.roll(u2, 255, 1)
        zm = pltpu.roll(u2, 1, 1)
        c0 = jnp.ones((8, 256), f32)
        for k, (u, p, q) in enumerate(((u0, xp, xm), (u1, yp, ym), (u2, zp, zm))):
            wp = h * (u + p)
            wm = h * (q + u)
            coef[2 * k, x] = -jnp.minimum(wp, 0.0)
            coef[2 * k + 1, x] = jnp.maximum(wm, 0.0)
            c0 = c0 - (jnp.maximum(wp, 0.0) - jnp.minimum(wm, 0.0))
        coef[6, x] = c0

    def group(i, c):
        gs = []
        for k in range(G):
            o = offs[0, i * G + k]
            t = o >> 7
            m = lane >= (o & 127)
            p = jnp.broadcast_to(pos[pl.ds(i * G + k, 1), :], (8, 128))
            q = p & 127
            there = p >= 0
            a = groups(d[t])
            b = groups(d[jnp.minimum(t + 1, 32)])
            gs.append([jnp.where(there, lane_gather(jnp.where(m, x, y), q), 0.0) for x, y in zip(a, b)])
        for k in range(G):
            flat[pl.ds(start_row(i, k), 56, stride=PITCH), :] = jnp.concatenate(gs[k], axis=0)
        return c

    lax.fori_loop(0, 128 // G, group, 0, unroll=2)

    def field(f, load, store):
        kd = kappa[f] * dt
        c6 = 6.0 * kd
        hyl = hyf[0, f]
        hyh = hyf[1, f]
        for x in range(8):
            v = load(x)
            xp = load(x + 1) if x < 7 else hxf[1, f]
            xm = load(x - 1) if x > 0 else hxf[0, f]
            yp = jnp.where(rows == 7, hyh[x:x + 1, :], pltpu.roll(v, 7, 0))
            ym = jnp.where(rows == 0, hyl[x:x + 1, :], pltpu.roll(v, 1, 0))
            zp = pltpu.roll(v, 255, 1)
            zm = pltpu.roll(v, 1, 1)
            acc = (coef[6, x] - c6) * v
            for k, nb in enumerate((xp, xm, yp, ym, zp, zm)):
                acc = acc + (coef[k, x] + kd) * nb
            store(x, acc + jnp.concatenate([ebuf[0, f, x], ebuf[1, f, x]], axis=1))

    def one(f, c):
        def st(x, v):
            obuf[f, x] = v
        field(f, lambda x: mix[f, x], st)
        pltpu.make_async_copy(obuf.at[f], out.at[f], sems.at[f]).start()
        return c

    def stt(x, v):
        obuf[53, x] = v
    field(53, lambda x: temp[x], stt)
    pltpu.make_async_copy(obuf.at[53], tout, sems.at[53]).start()
    lax.fori_loop(0, 53, one, 0)

    def drain(f, c):
        pltpu.make_async_copy(obuf.at[f], out.at[f], sems.at[f]).wait()
        return c
    lax.fori_loop(0, 53, drain, 0)
    pltpu.make_async_copy(obuf.at[53], tout, sems.at[53]).wait()


def finish(edges, offs, kappa, gm, pos, d, hx, hy, vel, temp, mix):
    return pl.pallas_call(
        functools.partial(finish_kernel, edges=edges),
        out_shape=(sd((53, 8, 8, 256), f32), sd((8, 8, 256), f32)),
        in_specs=[SMEM, SMEM] + [VMEM] * 9,
        out_specs=[HBM, HBM],
        scratch_shapes=[pltpu.VMEM((7, 8, 8, 256), f32), pltpu.VMEM((2, 56, 9, 8, 128), f32),
                        pltpu.VMEM((54, 8, 8, 256), f32), pltpu.VMEM((2, 56, 8, 256), f32),
                        pltpu.VMEM((2, 56, 8, 256), f32), dma((54,))],
        compiler_params=pltpu.CompilerParams(vmem_limit_bytes=24 << 20),
        name="finish",
    )(offs, kappa, kappa, gm, pos, d, hx, hy, vel, temp, mix)


def edges(nx, ny):
    gx, yz = lax.axis_index("gx"), lax.axis_index("yz")
    flag = lambda c: jnp.where(c, 1.0, 0.0).astype(f32)
    return flag(gx > 0), flag(gx < nx - 1), flag(yz > 0), flag(yz < ny - 1)


def shards(nx, ny, mix, temp, press, vel, kappa, tally, listing, *weights):
    packed, pos, offs, vmax, xs, ys = prep(tally, listing, mix, temp, press, vel)
    d, gm, hx, hy = chem(nx, ny, packed, vmax, xs, ys, *weights)
    return finish(functools.partial(edges, nx, ny), offs, kappa, gm, pos, d, hx, hy, vel, temp, mix)


def solution(mesh):
    in_specs = (
        P(None, "gx", "yz", None),
        P("gx", "yz", None),
        P("gx", "yz", None),
        P(None, "gx", "yz", None),
        P(),
        P("gx", "yz"),
        P("gx", "yz", None),
    ) + (P(),) * 10
    out_specs = (P(None, "gx", "yz", None), P("gx", "yz", None))
    nx, ny = mesh.shape["gx"], mesh.shape["yz"]
    return jax.shard_map(functools.partial(shards, nx, ny), mesh=mesh, in_specs=in_specs, out_specs=out_specs, check_vma=False)
```

time: 62 us -> 42.9 us (0.69)
  the two profiles are of different devices: /device:TPU:14 before, /device:TPU:1 now
where the time goes in v2:
time: 42.9 us; the launch traced here: 42.5 us
  Pallas kernels  40.8 us (95%)
  between operations  1.67 us (4%)
    pallas_call x1, Pallas kernels, chem(): pl.pallas_call(functools.partial(chem_kernel, nx=nx, ny=ny), out_shape=(s...  26.5 us
    pallas_call x1, Pallas kernels, finish(): pl.pallas_call(functools.partial(finish_kernel, edges=edges), out_shape=(...  9.84 us
    pallas_call x1, Pallas kernels, prep(): pl.pallas_call(prep_kernel, out_shape=(sd((33, 56, 128), f32), sd((128, 1...  4.49 us

profile of v2, /device:TPU:1, one launch (start us, length us, event | category | flops | bytes accessed | tf_op | source)
XLA Modules:
  0.0 42.5 jit_solution(15094052930250313609)
XLA Ops:
  0.6 0.0 copy-start.13
  0.6 0.0 copy-start.12
  0.7 0.0 copy-start.11
  0.7 0.0 copy-start.6
  0.7 0.0 copy-start.9
  0.7 0.0 copy-start.3
  0.7 0.0 copy-start.8
  0.7 0.0 copy-start.1
  0.7 0.0 copy-start.7
  0.7 0.0 copy-start.5
  1.5 4.5 %prep.1 = (f32[33,56,128]{2,1,0:T(8,128)S(1)}, s32[128,128]{1,0:T(8,128)S(1)}, s32[8,256]{1,0:T(8,128)S(1)}, f32[8,128]{1,0:T(8,128)S(1)}, bf16[2,448,256]{2,1,0...) custom-call(s32[1,1]{1,0:T(1,128)S(6)} %copy.19.tally, s32[1,1,4096]{2,1,0:T(1,128)} %listing.1, f32[53,8,8,256]{3,2,1,0:T(8,128)} %mix.3, ...), custom_call_target="tpu_custom_call" | custom-call | tf_op jit(solution)/shard_map/prep/pallas_call | solution.py:134
  6.0 0.0 copy-start
  6.0 0.0 copy-start.2
  6.1 0.0 copy-start.4
  6.1 0.0 copy-start.10
  6.1 0.0 copy-done.13
  6.1 0.0 copy-done.12
  6.1 0.0 copy-done.11
  6.1 0.0 copy-done.6
  6.1 0.0 copy-done.9
  6.1 0.0 copy-done.3
  6.1 0.0 copy-done.8
  6.2 26.5 %chem.1 = (f32[33,56,128]{2,1,0:T(8,128)S(1)}, f32[8,128]{1,0:T(8,128)S(1)}, bf16[2,448,256]{2,1,0:T(8,128)(2,1)S(1)}, bf16[2,448,256]{2,1,0:T(8,128)(2,1)S(1)}) custom-call(f32[33,56,128]{2,1,0:T(8,128)S(1)} %get-tuple-element.13.packed, f32[8,128]{1,0:T(8,128)S(1)} %get-tuple-element.14.vmax, bf16[2,448,256]{2,1,0:T(8,128)(2,1)S(1)} %get-tuple-element.15.xs, ...), custom_call_target="tpu_custom_call" | custom-call | tf_op jit(solution)/shard_map/chem/pallas_call | solution.py:244
  32.7 9.8 %finish.1 = (f32[53,8,8,256]{3,2,1,0:T(8,128)}, f32[8,8,256]{2,1,0:T(8,128)}) custom-call(s32[8,256]{1,0:T(8,128)S(1)} %get-tuple-element.12.offs, f32[54]{0:T(128)S(1)} %copy-done.10, f32[54]{0:T(128)S(1)} %copy-done.10, f32[8,128]{1,0:T(8,128)S(1)} %get-tuple-element.17.gm, s32[128,128]{1,0:T(8,128)S(1)} %get-tuple-element.18.pos, ...), custom_call_target="tpu_custom_call" | custom-call | tf_op jit(solution)/shard_map/finish/pallas_call | solution.py:349
  (7 shorter events, 0.0 us)
Async XLA Ops:
  0.6 5.4 %copy-start.13 = (f32[53]{0:T(128)S(1)}, f32[53]{0:T(128)}, u32[]{:S(2)}) copy-start(f32[53]{0:T(128)} %hr.1) | copy-start | bytes 640
  0.6 5.4 %copy-start.12 = (f32[53]{0:T(128)S(1)}, f32[53]{0:T(128)}, u32[]{:S(2)}) copy-start(f32[53]{0:T(128)} %inc.1) | copy-start | bytes 640
  0.7 5.4 %copy-start.11 = (f32[53]{0:T(128)S(1)}, f32[53]{0:T(128)}, u32[]{:S(2)}) copy-start(f32[53]{0:T(128)} %b4.1) | copy-start | bytes 640
  0.7 5.4 %copy-start.6 = (bf16[400,53]{0,1:T(8,128)(2,1)S(1)}, bf16[400,53]{0,1:T(8,128)(2,1)}, u32[]{:S(2)}) copy-start(bf16[400,53]{0,1:T(8,128)(2,1)} %param.30) | copy-start | bytes 127204
  0.7 5.4 %copy-start.9 = (f32[400]{0:T(512)S(1)}, f32[400]{0:T(512)}, u32[]{:S(2)}) copy-start(f32[400]{0:T(512)} %b3.1) | copy-start | bytes 4804
  0.7 5.4 %copy-start.3 = (bf16[800,400]{0,1:T(8,128)(2,1)S(1)}, bf16[800,400]{0,1:T(8,128)(2,1)}, u32[]{:S(2)}) copy-start(bf16[800,400]{0,1:T(8,128)(2,1)} %param.28) | copy-start | bytes 1920004
  0.7 5.4 %copy-start.8 = (f32[800]{0:T(1024)S(1)}, f32[800]{0:T(1024)}, u32[]{:S(2)}) copy-start(f32[800]{0:T(1024)} %b2.1) | copy-start | bytes 9604
  0.7 5.4 %copy-start.1 = (bf16[1600,800]{0,1:T(8,128)(2,1)S(1)}, bf16[1600,800]{0,1:T(8,128)(2,1)}, u32[]{:S(2)}) copy-start(bf16[1600,800]{0,1:T(8,128)(2,1)} %param.26) | copy-start | bytes 7680004
  0.7 5.4 %copy-start.7 = (f32[1600]{0:T(1024)S(1)}, f32[1600]{0:T(1024)}, u32[]{:S(2)}) copy-start(f32[1600]{0:T(1024)} %b1.1) | copy-start | bytes 19204
  0.7 5.4 %copy-start.5 = (bf16[55,1600]{1,0:T(8,128)(2,1)S(1)}, bf16[55,1600]{1,0:T(8,128)(2,1)}, u32[]{:S(2)}) copy-start(bf16[55,1600]{1,0:T(8,128)(2,1)} %w1.1) | copy-start | bytes 528004
  6.0 26.6 %copy-start = (f32[53,8,8,256]{3,2,1,0:T(8,128)S(1)}, f32[53,8,8,256]{3,2,1,0:T(8,128)}, u32[]{:S(2)}) copy-start(f32[53,8,8,256]{3,2,1,0:T(8,128)} %mix.3) | copy-start | bytes 10420228
  6.0 26.6 %copy-start.2 = (f32[3,8,8,256]{3,2,1,0:T(8,128)S(1)}, f32[3,8,8,256]{3,2,1,0:T(8,128)}, u32[]{:S(2)}) copy-start(f32[3,8,8,256]{3,2,1,0:T(8,128)} %vel.3) | copy-start | bytes 589828
  6.1 26.6 %copy-start.4 = (f32[8,8,256]{2,1,0:T(8,128)S(1)}, f32[8,8,256]{2,1,0:T(8,128)}, u32[]{:S(2)}) copy-start(f32[8,8,256]{2,1,0:T(8,128)} %temp.3) | copy-start | bytes 196612
  6.1 26.6 %copy-start.10 = (f32[54]{0:T(128)S(1)}, f32[54]{0:T(128)}, u32[]{:S(2)}) copy-start(f32[54]{0:T(128)} %kapv.1) | copy-start | bytes 652

commit v3 on v2

--- a/solution.py
+++ b/solution.py
@@ -20,6 +20,7 @@
 dma = pltpu.SemaphoreType.DMA
 G = 8
 NT = 8
+UF = 4
 PITCH = 72
 HALF = 56 * PITCH
 
@@ -199,7 +200,7 @@
     second = [remote(m1, s2.at[k], ssem2.at[k], rsem2.at[k], xpart[k]) for k in range(nx - 1)]
 
     def exchange(i):
-        @pl.when(i == 1)
+        @pl.when(i == 0)
         def _():
             pl.semaphore_wait(barrier, nx + ny - 2)
             for cp in first + halos:
@@ -257,8 +258,10 @@
     )(packed, vmax, xs, ys, w1, b1, w2.T, b2, w3.T, b3, w4.T, b4, inc, hr)
 
 
-def finish_kernel(offs, kappa, kapv, gm, pos, d, hx, hy, vel, temp, mix, out, tout,
-                  coef, ebuf, obuf, hxf, hyf, sems, *, edges):
+def finish_kernel(offs_in, kapv, gm, pos, d, hx, hy, vel, temp, mix, out, tout,
+                  coef, ebuf, obuf, hxf, hyf, kcol, offs, sems, osem, *, edges):
+    oc = pltpu.make_async_copy(offs_in, offs, osem)
+    oc.start()
     flat = ebuf.reshape(2 * HALF, 128)
     lo_x, hi_x, lo_y, hi_y = edges()
     rows = lax.broadcasted_iota(i32, (8, 256), 0)
@@ -266,7 +269,9 @@
     for k, (fx, fy) in enumerate(((lo_x, lo_y), (hi_x, hi_y))):
         hxf[k] = (hx[k].astype(f32) * fx).reshape(56, 8, 256)
         hyf[k] = (hy[k].astype(f32) * fy).reshape(56, 8, 256)
-    dt = 0.9 / (jnp.full((8, 256), jnp.max(gm[...])) + 6.0 * jnp.max(kapv[...].reshape(1, 54)))
+    kap = kapv[...].reshape(1, 54)
+    kcol[...] = col(jnp.concatenate([kap, jnp.zeros((1, 2), f32)], axis=1), 56)
+    dt = 0.9 / (jnp.full((8, 256), jnp.max(gm[...])) + 6.0 * jnp.max(kap))
     h = 0.5 * dt
     ux = [hxf[k, 54] + hxf[k, 55] for k in range(2)]
     uy = [hyf[k, 54] + hyf[k, 55] for k in range(2)]
@@ -289,6 +294,8 @@
             c0 = c0 - (jnp.maximum(wp, 0.0) - jnp.minimum(wm, 0.0))
         coef[6, x] = c0
 
+    oc.wait()
+
     def group(i, c):
         gs = []
         for k in range(G):
@@ -305,10 +312,10 @@
             flat[pl.ds(start_row(i, k), 56, stride=PITCH), :] = jnp.concatenate(gs[k], axis=0)
         return c
 
-    lax.fori_loop(0, 128 // G, group, 0, unroll=2)
+    lax.fori_loop(0, 128 // G, group, 0, unroll=4)
 
     def field(f, load, store):
-        kd = kappa[f] * dt
+        kd = jnp.concatenate([kcol[pl.ds(f, 1), :]] * 2, axis=1) * dt
         c6 = 6.0 * kd
         hyl = hyf[0, f]
         hyh = hyf[1, f]
@@ -336,7 +343,7 @@
         obuf[53, x] = v
     field(53, lambda x: temp[x], stt)
     pltpu.make_async_copy(obuf.at[53], tout, sems.at[53]).start()
-    lax.fori_loop(0, 53, one, 0)
+    lax.fori_loop(0, 53, one, 0, unroll=UF)
 
     def drain(f, c):
         pltpu.make_async_copy(obuf.at[f], out.at[f], sems.at[f]).wait()
@@ -349,14 +356,15 @@
     return pl.pallas_call(
         functools.partial(finish_kernel, edges=edges),
         out_shape=(sd((53, 8, 8, 256), f32), sd((8, 8, 256), f32)),
-        in_specs=[SMEM, SMEM] + [VMEM] * 9,
+        in_specs=[VMEM] * 10,
         out_specs=[HBM, HBM],
         scratch_shapes=[pltpu.VMEM((7, 8, 8, 256), f32), pltpu.VMEM((2, 56, 9, 8, 128), f32),
                         pltpu.VMEM((54, 8, 8, 256), f32), pltpu.VMEM((2, 56, 8, 256), f32),
-                        pltpu.VMEM((2, 56, 8, 256), f32), dma((54,))],
+                        pltpu.VMEM((2, 56, 8, 256), f32), pltpu.VMEM((56, 128), f32), pltpu.SMEM((8, 256), i32),
+                        dma((54,)), dma],
         compiler_params=pltpu.CompilerParams(vmem_limit_bytes=24 << 20),
         name="finish",
-    )(offs, kappa, kappa, gm, pos, d, hx, hy, vel, temp, mix)
+    )(offs, kappa, gm, pos, d, hx, hy, vel, temp, mix)
 
 
 def edges(nx, ny):

time: 42.9 us -> 38 us (0.89)
  Pallas kernels: 40.8 us -> 36.1 us
    pallas_call x1, Pallas kernels: 9.84 us -> 7.06 us  [finish(): pl.pallas_call(functools.partial(finish_kernel, edges=edges), out_shape=(...]
    pallas_call x1, Pallas kernels: 26.5 us -> 24.6 us  [chem(): pl.pallas_call(functools.partial(chem_kernel, nx=nx, ny=ny), out_shape=(s...]
where the time goes in v3:
time: 38 us; the launch traced here: 37.8 us
  Pallas kernels  36.1 us (95%)
  between operations  1.67 us (4%)
    pallas_call x1, Pallas kernels, chem(): pl.pallas_call(functools.partial(chem_kernel, nx=nx, ny=ny), out_shape=(s...  24.6 us
    pallas_call x1, Pallas kernels, finish(): pl.pallas_call(functools.partial(finish_kernel, edges=edges), out_shape=(...  7.06 us
    pallas_call x1, Pallas kernels, prep(): pl.pallas_call(prep_kernel, out_shape=(sd((33, 56, 128), f32), sd((128, 1...  4.49 us

profile of v3, /device:TPU:1, one launch (start us, length us, event | category | flops | bytes accessed | tf_op | source)
XLA Modules:
  0.0 37.8 jit_solution(1116491215008255466)
XLA Ops:
  0.6 0.0 copy-start.12
  0.6 0.0 copy-start.11
  0.7 0.0 copy-start.10
  0.7 0.0 copy-start.6
  0.7 0.0 copy-start.9
  0.7 0.0 copy-start.3
  0.7 0.0 copy-start.8
  0.7 0.0 copy-start.1
  0.7 0.0 copy-start.7
  0.7 0.0 copy-start.5
  1.5 4.5 %prep.1 = (f32[33,56,128]{2,1,0:T(8,128)S(1)}, s32[128,128]{1,0:T(8,128)S(1)}, s32[8,256]{1,0:T(8,128)S(1)}, f32[8,128]{1,0:T(8,128)S(1)}, bf16[2,448,256]{2,1,0...) custom-call(s32[1,1]{1,0:T(1,128)S(6)} %copy.19.tally, s32[1,1,4096]{2,1,0:T(1,128)} %listing.1, f32[53,8,8,256]{3,2,1,0:T(8,128)} %mix.3, ...), custom_call_target="tpu_custom_call" | custom-call | tf_op jit(solution)/shard_map/prep/pallas_call | solution.py:135
  6.0 0.0 copy-start
  6.0 0.0 copy-start.2
  6.1 0.0 copy-start.4
  6.1 0.0 copy-start.13
  6.1 0.0 copy-done.12
  6.1 0.0 copy-done.11
  6.1 0.0 copy-done.10
  6.1 0.0 copy-done.6
  6.1 0.0 copy-done.9
  6.1 0.0 copy-done.3
  6.1 0.0 copy-done.8
  6.2 24.6 %chem.1 = (f32[33,56,128]{2,1,0:T(8,128)S(1)}, f32[8,128]{1,0:T(8,128)S(1)}, bf16[2,448,256]{2,1,0:T(8,128)(2,1)S(1)}, bf16[2,448,256]{2,1,0:T(8,128)(2,1)S(1)}) custom-call(f32[33,56,128]{2,1,0:T(8,128)S(1)} %get-tuple-element.13.packed, f32[8,128]{1,0:T(8,128)S(1)} %get-tuple-element.14.vmax, bf16[2,448,256]{2,1,0:T(8,128)(2,1)S(1)} %get-tuple-element.15.xs, ...), custom_call_target="tpu_custom_call" | custom-call | tf_op jit(solution)/shard_map/chem/pallas_call | solution.py:245
  30.8 7.1 %finish.1 = (f32[53,8,8,256]{3,2,1,0:T(8,128)}, f32[8,8,256]{2,1,0:T(8,128)}) custom-call(s32[8,256]{1,0:T(8,128)S(1)} %get-tuple-element.12.offs_in, f32[54]{0:T(128)S(1)} %copy-done.13, f32[8,128]{1,0:T(8,128)S(1)} %get-tuple-element.17.gm, s32[128,128]{1,0:T(8,128)S(1)} %get-tuple-element.18.pos, f32[33,56,128]{2,1,0:T(8,128)S(1)} %get-tuple-element.19.d, ...), custom_call_target="tpu_custom_call" | custom-call | tf_op jit(solution)/shard_map/finish/pallas_call | solution.py:356
  (7 shorter events, 0.0 us)
Async XLA Ops:
  0.6 5.4 %copy-start.12 = (f32[53]{0:T(128)S(1)}, f32[53]{0:T(128)}, u32[]{:S(2)}) copy-start(f32[53]{0:T(128)} %hr.1) | copy-start | bytes 640
  0.6 5.4 %copy-start.11 = (f32[53]{0:T(128)S(1)}, f32[53]{0:T(128)}, u32[]{:S(2)}) copy-start(f32[53]{0:T(128)} %inc.1) | copy-start | bytes 640
  0.7 5.4 %copy-start.10 = (f32[53]{0:T(128)S(1)}, f32[53]{0:T(128)}, u32[]{:S(2)}) copy-start(f32[53]{0:T(128)} %b4.1) | copy-start | bytes 640
  0.7 5.4 %copy-start.6 = (bf16[400,53]{0,1:T(8,128)(2,1)S(1)}, bf16[400,53]{0,1:T(8,128)(2,1)}, u32[]{:S(2)}) copy-start(bf16[400,53]{0,1:T(8,128)(2,1)} %param.30) | copy-start | bytes 127204
  0.7 5.4 %copy-start.9 = (f32[400]{0:T(512)S(1)}, f32[400]{0:T(512)}, u32[]{:S(2)}) copy-start(f32[400]{0:T(512)} %b3.1) | copy-start | bytes 4804
  0.7 5.4 %copy-start.3 = (bf16[800,400]{0,1:T(8,128)(2,1)S(1)}, bf16[800,400]{0,1:T(8,128)(2,1)}, u32[]{:S(2)}) copy-start(bf16[800,400]{0,1:T(8,128)(2,1)} %param.28) | copy-start | bytes 1920004
  0.7 5.4 %copy-start.8 = (f32[800]{0:T(1024)S(1)}, f32[800]{0:T(1024)}, u32[]{:S(2)}) copy-start(f32[800]{0:T(1024)} %b2.1) | copy-start | bytes 9604
  0.7 5.4 %copy-start.1 = (bf16[1600,800]{0,1:T(8,128)(2,1)S(1)}, bf16[1600,800]{0,1:T(8,128)(2,1)}, u32[]{:S(2)}) copy-start(bf16[1600,800]{0,1:T(8,128)(2,1)} %param.26) | copy-start | bytes 7680004
  0.7 5.4 %copy-start.7 = (f32[1600]{0:T(1024)S(1)}, f32[1600]{0:T(1024)}, u32[]{:S(2)}) copy-start(f32[1600]{0:T(1024)} %b1.1) | copy-start | bytes 19204
  0.7 5.4 %copy-start.5 = (bf16[55,1600]{1,0:T(8,128)(2,1)S(1)}, bf16[55,1600]{1,0:T(8,128)(2,1)}, u32[]{:S(2)}) copy-start(bf16[55,1600]{1,0:T(8,128)(2,1)} %w1.1) | copy-start | bytes 528004
  6.0 24.7 %copy-start = (f32[53,8,8,256]{3,2,1,0:T(8,128)S(1)}, f32[53,8,8,256]{3,2,1,0:T(8,128)}, u32[]{:S(2)}) copy-start(f32[53,8,8,256]{3,2,1,0:T(8,128)} %mix.3) | copy-start | bytes 10420228
  6.0 24.7 %copy-start.2 = (f32[3,8,8,256]{3,2,1,0:T(8,128)S(1)}, f32[3,8,8,256]{3,2,1,0:T(8,128)}, u32[]{:S(2)}) copy-start(f32[3,8,8,256]{3,2,1,0:T(8,128)} %vel.3) | copy-start | bytes 589828
  6.1 24.7 %copy-start.4 = (f32[8,8,256]{2,1,0:T(8,128)S(1)}, f32[8,8,256]{2,1,0:T(8,128)}, u32[]{:S(2)}) copy-start(f32[8,8,256]{2,1,0:T(8,128)} %temp.3) | copy-start | bytes 196612
  6.1 24.7 %copy-start.13 = (f32[54]{0:T(128)S(1)}, f32[54]{0:T(128)}, u32[]{:S(2)}) copy-start(f32[54]{0:T(128)} %kapv.1) | copy-start | bytes 652

commit v4 on v3

--- a/solution.py
+++ b/solution.py
@@ -18,7 +18,7 @@
 HBM = pl.BlockSpec(memory_space=pltpu.HBM)
 sd = jax.ShapeDtypeStruct
 dma = pltpu.SemaphoreType.DMA
-G = 8
+G = 16
 NT = 8
 UF = 4
 PITCH = 72
@@ -108,7 +108,7 @@
             cur = [jnp.where(fresh, g, c) for g, c in zip(gs[k], cur)]
         return tuple(cur)
 
-    cur = lax.fori_loop(0, 128 // G, group, tuple(jnp.zeros((8, 128), f32) for _ in range(7)), unroll=4)
+    cur = lax.fori_loop(0, 128 // G, group, tuple(jnp.zeros((8, 128), f32) for _ in range(7)), unroll=8)
     for q in range(7):
         packed[n >> 7, 8 * q:8 * q + 8] = cur[q]
     for k, x in enumerate((0, 7)):
@@ -196,22 +196,22 @@
              remote(ys.at[0], hy.at[1], hsend.at[1], hrecv.at[1], down_y),
              remote(xs.at[1], hx.at[0], hsend.at[2], hrecv.at[2], up_x),
              remote(xs.at[0], hx.at[1], hsend.at[3], hrecv.at[3], down_x)]
-    first = [remote(vmax, s1.at[k], ssem1.at[k], rsem1.at[k], ypart[k]) for k in range(ny - 1)]
-    second = [remote(m1, s2.at[k], ssem2.at[k], rsem2.at[k], xpart[k]) for k in range(nx - 1)]
+    first = [remote(vmax, s1.at[k], ssem1.at[k], rsem1.at[k], xpart[k]) for k in range(nx - 1)]
+    second = [remote(m1, s2.at[k], ssem2.at[k], rsem2.at[k], ypart[k]) for k in range(ny - 1)]
 
     def exchange(i):
         @pl.when(i == 0)
         def _():
             pl.semaphore_wait(barrier, nx + ny - 2)
-            for cp in first + halos:
+            for cp in first + halos[:2]:
                 cp.start()
 
-        @pl.when(i == 2)
+        @pl.when(i == 1)
         def _():
             for cp in first:
                 cp.wait()
             m1[...] = jnp.maximum(vmax[...], jnp.max(s1[...], axis=0))
-            for cp in second:
+            for cp in second + halos[2:]:
                 cp.start()
 
     def block(i, c):
@@ -250,8 +250,8 @@
         scratch_shapes=[
             pltpu.VMEM((1600, 64), bf), pltpu.VMEM((800, 128), f32), pltpu.VMEM((400, 128), f32),
             pltpu.VMEM((3, 56, 128), f32),
-            pltpu.VMEM((ny - 1, 8, 128), f32), pltpu.VMEM((nx - 1, 8, 128), f32), pltpu.VMEM((8, 128), f32),
-            dma((ny - 1,)), dma((ny - 1,)), dma((nx - 1,)), dma((nx - 1,)), dma((4,)), dma((4,)),
+            pltpu.VMEM((nx - 1, 8, 128), f32), pltpu.VMEM((ny - 1, 8, 128), f32), pltpu.VMEM((8, 128), f32),
+            dma((nx - 1,)), dma((nx - 1,)), dma((ny - 1,)), dma((ny - 1,)), dma((4,)), dma((4,)),
         ],
         compiler_params=pltpu.CompilerParams(vmem_limit_bytes=32 << 20, collective_id=0, has_side_effects=True),
         name="chem",
@@ -312,7 +312,7 @@
             flat[pl.ds(start_row(i, k), 56, stride=PITCH), :] = jnp.concatenate(gs[k], axis=0)
         return c
 
-    lax.fori_loop(0, 128 // G, group, 0, unroll=4)
+    lax.fori_loop(0, 128 // G, group, 0, unroll=2)
 
     def field(f, load, store):
         kd = jnp.concatenate([kcol[pl.ds(f, 1), :]] * 2, axis=1) * dt

time: 38 us -> 37.7 us (level)
  no operation moved by 1% of the time
where the time goes in v4:
time: 37.7 us; the launch traced here: 37.6 us
  Pallas kernels  35.8 us (95%)
  between operations  1.67 us (4%)
    pallas_call x1, Pallas kernels, chem(): pl.pallas_call(functools.partial(chem_kernel, nx=nx, ny=ny), out_shape=(s...  24.5 us
    pallas_call x1, Pallas kernels, finish(): pl.pallas_call(functools.partial(finish_kernel, edges=edges), out_shape=(...  7.06 us
    pallas_call x1, Pallas kernels, prep(): pl.pallas_call(prep_kernel, out_shape=(sd((33, 56, 128), f32), sd((128, 1...  4.23 us

profile of v4, /device:TPU:1, one launch (start us, length us, event | category | flops | bytes accessed | tf_op | source)
XLA Modules:
  0.0 37.6 jit_solution(873214550243519539)
XLA Ops:
  0.6 0.0 copy-start.12
  0.6 0.0 copy-start.11
  0.7 0.0 copy-start.10
  0.7 0.0 copy-start.6
  0.7 0.0 copy-start.9
  0.7 0.0 copy-start.3
  0.7 0.0 copy-start.8
  0.7 0.0 copy-start.1
  0.7 0.0 copy-start.7
  0.7 0.0 copy-start.5
  1.5 4.2 %prep.1 = (f32[33,56,128]{2,1,0:T(8,128)S(1)}, s32[128,128]{1,0:T(8,128)S(1)}, s32[8,256]{1,0:T(8,128)S(1)}, f32[8,128]{1,0:T(8,128)S(1)}, bf16[2,448,256]{2,1,0...) custom-call(s32[1,1]{1,0:T(1,128)S(6)} %copy.19.tally, s32[1,1,4096]{2,1,0:T(1,128)} %listing.1, f32[53,8,8,256]{3,2,1,0:T(8,128)} %mix.3, ...), custom_call_target="tpu_custom_call" | custom-call | tf_op jit(solution)/shard_map/prep/pallas_call | solution.py:135
  5.8 0.0 copy-start
  5.8 0.0 copy-start.2
  5.8 0.0 copy-start.4
  5.8 0.0 copy-start.13
  5.8 0.0 copy-done.12
  5.8 0.0 copy-done.11
  5.8 0.0 copy-done.10
  5.8 0.0 copy-done.6
  5.9 0.0 copy-done.9
  5.9 0.0 copy-done.3
  5.9 0.0 copy-done.8
  5.9 24.5 %chem.1 = (f32[33,56,128]{2,1,0:T(8,128)S(1)}, f32[8,128]{1,0:T(8,128)S(1)}, bf16[2,448,256]{2,1,0:T(8,128)(2,1)S(1)}, bf16[2,448,256]{2,1,0:T(8,128)(2,1)S(1)}) custom-call(f32[33,56,128]{2,1,0:T(8,128)S(1)} %get-tuple-element.13.packed, f32[8,128]{1,0:T(8,128)S(1)} %get-tuple-element.14.vmax, bf16[2,448,256]{2,1,0:T(8,128)(2,1)S(1)} %get-tuple-element.15.xs, ...), custom_call_target="tpu_custom_call" | custom-call | tf_op jit(solution)/shard_map/chem/pallas_call | solution.py:245
  30.5 7.1 %finish.1 = (f32[53,8,8,256]{3,2,1,0:T(8,128)}, f32[8,8,256]{2,1,0:T(8,128)}) custom-call(s32[8,256]{1,0:T(8,128)S(1)} %get-tuple-element.12.offs_in, f32[54]{0:T(128)S(1)} %copy-done.13, f32[8,128]{1,0:T(8,128)S(1)} %get-tuple-element.17.gm, s32[128,128]{1,0:T(8,128)S(1)} %get-tuple-element.18.pos, f32[33,56,128]{2,1,0:T(8,128)S(1)} %get-tuple-element.19.d, ...), custom_call_target="tpu_custom_call" | custom-call | tf_op jit(solution)/shard_map/finish/pallas_call | solution.py:356
  (7 shorter events, 0.0 us)
Async XLA Ops:
  0.6 5.2 %copy-start.12 = (f32[53]{0:T(128)S(1)}, f32[53]{0:T(128)}, u32[]{:S(2)}) copy-start(f32[53]{0:T(128)} %hr.1) | copy-start | bytes 640
  0.6 5.2 %copy-start.11 = (f32[53]{0:T(128)S(1)}, f32[53]{0:T(128)}, u32[]{:S(2)}) copy-start(f32[53]{0:T(128)} %inc.1) | copy-start | bytes 640
  0.7 5.2 %copy-start.10 = (f32[53]{0:T(128)S(1)}, f32[53]{0:T(128)}, u32[]{:S(2)}) copy-start(f32[53]{0:T(128)} %b4.1) | copy-start | bytes 640
  0.7 5.2 %copy-start.6 = (bf16[400,53]{0,1:T(8,128)(2,1)S(1)}, bf16[400,53]{0,1:T(8,128)(2,1)}, u32[]{:S(2)}) copy-start(bf16[400,53]{0,1:T(8,128)(2,1)} %param.30) | copy-start | bytes 127204
  0.7 5.2 %copy-start.9 = (f32[400]{0:T(512)S(1)}, f32[400]{0:T(512)}, u32[]{:S(2)}) copy-start(f32[400]{0:T(512)} %b3.1) | copy-start | bytes 4804
  0.7 5.2 %copy-start.3 = (bf16[800,400]{0,1:T(8,128)(2,1)S(1)}, bf16[800,400]{0,1:T(8,128)(2,1)}, u32[]{:S(2)}) copy-start(bf16[800,400]{0,1:T(8,128)(2,1)} %param.28) | copy-start | bytes 1920004
  0.7 5.2 %copy-start.8 = (f32[800]{0:T(1024)S(1)}, f32[800]{0:T(1024)}, u32[]{:S(2)}) copy-start(f32[800]{0:T(1024)} %b2.1) | copy-start | bytes 9604
  0.7 5.2 %copy-start.1 = (bf16[1600,800]{0,1:T(8,128)(2,1)S(1)}, bf16[1600,800]{0,1:T(8,128)(2,1)}, u32[]{:S(2)}) copy-start(bf16[1600,800]{0,1:T(8,128)(2,1)} %param.26) | copy-start | bytes 7680004
  0.7 5.2 %copy-start.7 = (f32[1600]{0:T(1024)S(1)}, f32[1600]{0:T(1024)}, u32[]{:S(2)}) copy-start(f32[1600]{0:T(1024)} %b1.1) | copy-start | bytes 19204
  0.7 5.2 %copy-start.5 = (bf16[55,1600]{1,0:T(8,128)(2,1)S(1)}, bf16[55,1600]{1,0:T(8,128)(2,1)}, u32[]{:S(2)}) copy-start(bf16[55,1600]{1,0:T(8,128)(2,1)} %w1.1) | copy-start | bytes 528004
  5.8 24.7 %copy-start = (f32[53,8,8,256]{3,2,1,0:T(8,128)S(1)}, f32[53,8,8,256]{3,2,1,0:T(8,128)}, u32[]{:S(2)}) copy-start(f32[53,8,8,256]{3,2,1,0:T(8,128)} %mix.3) | copy-start | bytes 10420228
  5.8 24.7 %copy-start.2 = (f32[3,8,8,256]{3,2,1,0:T(8,128)S(1)}, f32[3,8,8,256]{3,2,1,0:T(8,128)}, u32[]{:S(2)}) copy-start(f32[3,8,8,256]{3,2,1,0:T(8,128)} %vel.3) | copy-start | bytes 589828
  5.8 24.7 %copy-start.4 = (f32[8,8,256]{2,1,0:T(8,128)S(1)}, f32[8,8,256]{2,1,0:T(8,128)}, u32[]{:S(2)}) copy-start(f32[8,8,256]{2,1,0:T(8,128)} %temp.3) | copy-start | bytes 196612
  5.8 24.7 %copy-start.13 = (f32[54]{0:T(128)S(1)}, f32[54]{0:T(128)}, u32[]{:S(2)}) copy-start(f32[54]{0:T(128)} %kapv.1) | copy-start | bytes 652
